TPU v7x, 512 devices: a whole 4x4x16 slice. The times are simulated.
512 devices in a mesh: dp: 8 (over y, core), tile: 64 (over x, z).
Axes of the slice: x: 4, y: 4, z: 16, core: 2. Of those that a mesh axis runs over, the one named last changes fastest.
Arguments:
- tokens: bfloat16 [65536, 2048], P(('dp', 'tile')), may hold values from -6 to 6
- expert_ids: int32 [65536, 8], P(('dp', 'tile')), may hold values from 0 to 127, all different within a row; in each aligned block of 128 rows (0 to 127, 128 to 255, ...) at most 10 rows name the same one
- gates: float32 [65536, 8], P(('dp', 'tile')), may hold values from 0.05 to 1
- tile_slot: int32 [60], replicated, may hold values from 0 to 63, as said below
- w_gate: bfloat16 [64, 2048, 128], P('tile'), may hold values from -0.125 to 0.125
- w_up: bfloat16 [64, 2048, 128], P('tile'), may hold values from -0.125 to 0.125
- w_down: bfloat16 [64, 128, 2048], P('tile'), may hold values from -0.21875 to 0.21875
- grad_out: bfloat16 [65536, 2048], P(('dp', 'tile')), may hold values from -6 to 6
Outputs:
- layer_out: bfloat16 [65536, 2048], P(('dp', 'tile'))
- token_grads: bfloat16 [65536, 2048], P(('dp', 'tile'))
- gate_grads: float32 [65536, 8], P(('dp', 'tile'))
- gate_weight_grads: bfloat16 [64, 2048, 128], P('tile', 'dp')
- up_weight_grads: bfloat16 [64, 2048, 128], P('tile', 'dp')
- down_weight_grads: bfloat16 [64, 128, 2048], P('tile', None, 'dp')
Inputs may be any that keep to these rules, and one draw needn't show every extreme that they name: `expert_ids`: each row names 8 different experts; the 128 rows of one device name one expert at most 10 times. `tile_slot`: all entries differ.
All inputs are finite; a program needn't handle non-finite values.
Results may differ from a plain program's by a relative error of at most 0.017.
Values may be sent and summed in bfloat16 or wider, within the bound.
No kernel may reach another device: no remote copies, remote signals or barrier semaphores. Data moves between devices by JAX's collectives and lax.ppermute only.
A program may use at most 64 MiB of HBM per device.

v0:
```python
import jax
import jax.numpy as jnp
from jax import lax
from jax.sharding import PartitionSpec as P

D = 2048
TOPK = 8
TILE_W = 128
HTILES = 6
CAP = 10


def tile_backward(scaled_flat, pre_gate, pre_up, weight_gate, weight_up, weight_down):
    contract_cols = (((1,), (1,)), ((), ()))
    sigmoid_gate = jax.nn.sigmoid(pre_gate)
    activated = pre_gate * sigmoid_gate
    hidden = (activated * pre_up).astype(jnp.bfloat16)
    hidden_grad = lax.dot_general(
        scaled_flat, weight_down, contract_cols, preferred_element_type=jnp.float32
    )
    up_pre_grad = (hidden_grad * activated).astype(jnp.bfloat16)
    gate_pre_grad = (
        hidden_grad * pre_up * sigmoid_gate * (1.0 + pre_gate * (1.0 - sigmoid_gate))
    ).astype(jnp.bfloat16)
    tile_in = lax.dot_general(
        gate_pre_grad, weight_gate, contract_cols, preferred_element_type=jnp.float32
    )
    tile_in = tile_in + lax.dot_general(
        up_pre_grad, weight_up, contract_cols, preferred_element_type=jnp.float32
    )
    return (hidden, up_pre_grad, gate_pre_grad, tile_in.astype(jnp.bfloat16))


def per_device(tokens, expert_ids, gates, tile_slot, w_gate, w_up, w_down, grad_out):
    tile_count = lax.axis_size("tile")
    tok_rows = tokens.shape[0]
    window_experts = tile_slot.shape[0] // HTILES
    slot_count = window_experts * CAP
    weight_gate = w_gate[0]
    weight_up = w_up[0]
    weight_down = w_down[0]
    contract_rows = (((0,), (0,)), ((), ()))
    route_ids = expert_ids.reshape(-1)
    member = (route_ids[:, None] == jnp.arange(window_experts, dtype=jnp.int32)[None, :]).astype(
        jnp.int32
    )
    slot_rank = jnp.sum((jnp.cumsum(member, axis=0) - member) * member, axis=1)
    position = jnp.where(route_ids < window_experts, route_ids * CAP + slot_rank, slot_count)
    choose = (position[:, None] == jnp.arange(slot_count, dtype=jnp.int32)[None, :]).astype(
        jnp.float32
    )
    picker = jnp.sum(choose.reshape(tok_rows, TOPK, slot_count), axis=1)
    picker_half = picker.astype(jnp.bfloat16)
    expert_rows = lax.dot_general(
        picker_half, tokens, contract_rows, preferred_element_type=jnp.float32
    ).astype(jnp.bfloat16)
    gate_slot = jnp.dot(gates.reshape(-1), choose, precision=lax.Precision.HIGHEST)
    placed = tile_slot.reshape(window_experts, HTILES)
    owners = jnp.arange(tile_count, dtype=jnp.int32)[:, None, None]
    holder = jnp.sum((placed[None, :, :] == owners).astype(jnp.float32), axis=2).astype(
        jnp.bfloat16
    )

    def spread(values):
        blocks = values.reshape(window_experts, CAP, D)
        return jnp.einsum("je,ecd->jcd", holder, blocks, preferred_element_type=jnp.float32).astype(
            jnp.bfloat16
        )

    def collect(values):
        summed = jnp.einsum("je,jcd->ecd", holder, values, preferred_element_type=jnp.float32)
        return summed.reshape(slot_count, D)

    sent_rows = spread(expert_rows)
    upstream = lax.dot_general(
        picker_half, grad_out, contract_rows, preferred_element_type=jnp.float32
    )
    scaled = (gate_slot[:, None] * upstream).astype(jnp.bfloat16)
    scaled_sent = spread(scaled)
    received = lax.all_to_all(sent_rows, "tile", split_axis=0, concat_axis=0, tiled=True)
    count = received.shape[1]
    flat_rows = received.reshape(-1, D)
    pre_gate = jnp.dot(flat_rows, weight_gate, preferred_element_type=jnp.float32)
    pre_up = jnp.dot(flat_rows, weight_up, preferred_element_type=jnp.float32)
    hidden = (jax.nn.silu(pre_gate) * pre_up).astype(jnp.bfloat16)
    partial_value = jnp.dot(hidden, weight_down, preferred_element_type=jnp.float32).astype(
        jnp.bfloat16
    )
    returned = lax.all_to_all(
        partial_value.reshape(tile_count, count, D), "tile", split_axis=0, concat_axis=0, tiled=True
    )
    returned, kept_rows, kept_gate, kept_up = (
        returned,
        received,
        pre_gate.reshape(tile_count, count, TILE_W),
        pre_up.reshape(tile_count, count, TILE_W),
    )
    expert_out = collect(returned)
    input_back, scaled_rows = (
        lax.all_to_all(sent_rows, "tile", split_axis=0, concat_axis=0, tiled=True),
        lax.all_to_all(scaled_sent, "tile", split_axis=0, concat_axis=0, tiled=True),
    )
    input_rows = input_back.reshape(-1, D)
    pre_gate = jnp.dot(input_rows, weight_gate, preferred_element_type=jnp.float32)
    pre_up = jnp.dot(input_rows, weight_up, preferred_element_type=jnp.float32)
    scaled_flat = scaled_rows.reshape(-1, D)
    hidden, up_pre_grad, gate_pre_grad, tile_in = tile_backward(
        scaled_flat, pre_gate, pre_up, weight_gate, weight_up, weight_down
    )
    input_back_rows = lax.all_to_all(
        tile_in.reshape(tile_count, -1, D), "tile", split_axis=0, concat_axis=0, tiled=True
    )
    layer_out = jnp.dot(
        picker, gate_slot[:, None] * expert_out, precision=lax.Precision.HIGHEST
    ).astype(jnp.bfloat16)
    gate_terms = jnp.sum(expert_out * upstream, axis=1)
    gate_grads = jnp.dot(choose, gate_terms, precision=lax.Precision.HIGHEST).reshape(
        tok_rows, TOPK
    )
    input_slot = collect(input_back_rows)
    token_grads = jnp.dot(picker, input_slot, precision=lax.Precision.HIGHEST).astype(jnp.bfloat16)
    grad_gate = lax.dot_general(
        input_rows, gate_pre_grad, contract_rows, preferred_element_type=jnp.float32
    )
    grad_up = lax.dot_general(
        input_rows, up_pre_grad, contract_rows, preferred_element_type=jnp.float32
    )
    grad_down = lax.dot_general(
        hidden, scaled_flat, contract_rows, preferred_element_type=jnp.float32
    )
    summed_gate, summed_up, summed_down = (
        lax.psum_scatter(
            grad_gate.astype(jnp.bfloat16), "dp", scatter_dimension=0, tiled=True
        ).astype(jnp.float32),
        lax.psum_scatter(
            grad_up.astype(jnp.bfloat16), "dp", scatter_dimension=0, tiled=True
        ).astype(jnp.float32),
        lax.psum_scatter(
            grad_down.astype(jnp.bfloat16), "dp", scatter_dimension=1, tiled=True
        ).astype(jnp.float32),
    )
    gate_weight_grads = summed_gate.astype(jnp.bfloat16)[None]
    up_weight_grads = summed_up.astype(jnp.bfloat16)[None]
    down_weight_grads = summed_down.astype(jnp.bfloat16)[None]
    return (
        layer_out,
        token_grads,
        gate_grads,
        gate_weight_grads,
        up_weight_grads,
        down_weight_grads,
    )


def solution(mesh):
    in_specs = (
        P(("dp", "tile"), None),
        P(("dp", "tile"), None),
        P(("dp", "tile"), None),
        P(),
        P("tile", None, None),
        P("tile", None, None),
        P("tile", None, None),
        P(("dp", "tile"), None),
    )
    out_specs = (
        P(("dp", "tile"), None),
        P(("dp", "tile"), None),
        P(("dp", "tile"), None),
        P("tile", "dp", None),
        P("tile", "dp", None),
        P("tile", None, "dp"),
    )
    return jax.shard_map(
        per_device, mesh=mesh, in_specs=in_specs, out_specs=out_specs, check_vma=False
    )
```

profile of v0, /device:TPU:1, one launch (start us, length us, event | category | flops | bytes accessed | tf_op | source)
XLA Modules:
  0.0 871.7 jit_solution(9343855344934412784)
XLA Ops:
  9.1 2.8 reduce-window.6
  15.7 2.0 convolution_convert_fusion.1
  19.2 203.7 %all_to_all.21 = bf16[64,10,2048]{2,1,0:T(8,128)(2,1)} all-to-all(bf16[64,10,2048]{2,1,0:T(8,128)(2,1)S(1)} %copy.80), channel_id=1, replica_groups=mesh['dp'=8,'tile'=64] {'tile'}, dimensions={0} | all-to-all | bytes 5242880 | tf_op jit(solution)/shard_map/all_to_all | solution.py:80
  222.9 4.1 reshape.96
  227.0 1.9 fusion.15
  231.2 2.4 convolution_convert_fusion.2
  233.6 5.4 reshape.97
  239.0 11.4 %all-to-all-start.1 = ((bf16[64,10,2048]{2,1,0:T(8,128)(2,1)}), bf16[64,10,2048]{2,1,0:T(8,128)(2,1)}, u32[]{:S(2)}, u32[]{:S(2)}) async-start(bf16[64,10,2048]{2,1,0:T(8,128)(2,1)} %reshape.97), calls=%async_computation.1 | async-start | bytes 8388608 | tf_op jit(solution)/shard_map/all_to_all | solution.py:89
  252.5 180.3 %all-to-all-done.1 = bf16[64,10,2048]{2,1,0:T(8,128)(2,1)} async-done(((bf16[64,10,2048]{2,1,0:T(8,128)(2,1)}), bf16[64,10,2048]{2,1,0:T(8,128)(2,1)}, u32[]{:S(2)}, u32[]{:S(2)}) %all-to-all-start.1) | async-done | bytes 2621472 | tf_op jit(solution)/shard_map/all_to_all | solution.py:89
  432.8 5.1 fusion.2
  439.4 2.3 reshape.98
  441.7 2.4 multiply_reduce_fusion
  444.2 2.0 reshape.99
  446.2 2.0 convolution_convert_fusion
  449.8 194.0 %all_to_all.22 = bf16[64,10,2048]{2,1,0:T(8,128)(2,1)} all-to-all(bf16[64,10,2048]{2,1,0:T(8,128)(2,1)S(1)} %copy.84), channel_id=1, replica_groups=mesh['dp'=8,'tile'=64] {'tile'}, dimensions={0} | all-to-all | bytes 5242880 | tf_op jit(solution)/shard_map/all_to_all | solution.py:101
  643.8 5.5 reshape.100
  649.3 2.7 multiply_convert_fusion.1
  653.2 2.4 add_convert_fusion
  655.6 5.4 reshape.101
  660.9 14.2 %all-to-all-start.3 = ((bf16[64,10,2048]{2,1,0:T(8,128)(2,1)}), bf16[64,10,2048]{2,1,0:T(8,128)(2,1)}, u32[]{:S(2)}, u32[]{:S(2)}) async-start(bf16[64,10,2048]{2,1,0:T(8,128)(2,1)} %reshape.101), calls=%async_computation.3 | async-start | bytes 8388608 | tf_op jit(solution)/shard_map/all_to_all | solution.py:110
  675.5 3.1 convolution_convert_fusion.3
  683.2 3.0 convolution_convert_fusion.7
  686.2 171.4 %all-to-all-done.3 = bf16[64,10,2048]{2,1,0:T(8,128)(2,1)} async-done(((bf16[64,10,2048]{2,1,0:T(8,128)(2,1)}), bf16[64,10,2048]{2,1,0:T(8,128)(2,1)}, u32[]{:S(2)}, u32[]{:S(2)}) %all-to-all-start.3) | async-done | bytes 2621472 | tf_op jit(solution)/shard_map/all_to_all | solution.py:110
  857.6 5.1 fusion
  (68 shorter events, 23.0 us)
Async XLA Ops:
  7.2 224.1 %copy-start = (bf16[1,128,2048]{2,1,0:T(8,128)(2,1)S(1)}, bf16[1,128,2048]{2,1,0:T(8,128)(2,1)}, u32[]{:S(2)}) copy-start(bf16[1,128,2048]{2,1,0:T(8,128)(2,1)} %param.14) | copy-start | bytes 1572868
  227.0 2.0 copy-start.8
  230.6 0.7 copy-start.2
  239.0 11.4 %copy-start.10 = (f32[128,8]{0,1:T(8,128)S(1)}, f32[128,8]{0,1:T(8,128)}, u32[]{:S(2)}) copy-start(f32[128,8]{0,1:T(8,128)} %param.10) | copy-start | bytes 12292
  239.0 193.8 %all-to-all-start.1 = ((bf16[64,10,2048]{2,1,0:T(8,128)(2,1)}), bf16[64,10,2048]{2,1,0:T(8,128)(2,1)}, u32[]{:S(2)}, u32[]{:S(2)}) async-start(bf16[64,10,2048]{2,1,0:T(8,128)(2,1)} %reshape.97), calls=%async_computation.1 | async-start | bytes 8388608 | tf_op jit(solution)/shard_map/all_to_all | solution.py:89
  649.3 2.7 copy-start.1
  652.0 0.9 copy-start.4
  652.0 0.9 copy-start.6
  652.0 1.1 copy-start.9
  660.9 14.5 %copy-start.3 = (bf16[640,128]{1,0:T(8,128)(2,1)S(1)}, bf16[640,128]{1,0:T(8,128)(2,1)}, u32[]{:S(2)}) copy-start(bf16[640,128]{1,0:T(8,128)(2,1)} %copy-done.2) | copy-start | bytes 491524
  660.9 196.7 %all-to-all-start.3 = ((bf16[64,10,2048]{2,1,0:T(8,128)(2,1)}), bf16[64,10,2048]{2,1,0:T(8,128)(2,1)}, u32[]{:S(2)}, u32[]{:S(2)}) async-start(bf16[64,10,2048]{2,1,0:T(8,128)(2,1)} %reshape.101), calls=%async_computation.3 | async-start | bytes 8388608 | tf_op jit(solution)/shard_map/all_to_all | solution.py:110
  675.2 3.5 copy-start.5
  675.2 190.0 %reduce-scatter.8.cloned.1.call-start = ((), (), s32[]{:S(2)}) async-start(), calls=%async_computation.9 | async-start | bytes 589824 | tf_op jit(solution)/shard_map/reduce_scatter | solution.py:138
  678.6 1.9 copy-start.7
  678.7 186.5 %reduce-scatter.4.cloned.1.call-start = ((), (), s32[]{:S(2)}) async-start(), calls=%async_computation.7 | async-start | bytes 589824 | tf_op jit(solution)/shard_map/reduce_scatter | solution.py:132
  680.5 184.7 %reduce-scatter.6.cloned.1.call-start = ((), (), s32[]{:S(2)}) async-start(), calls=%async_computation.8 | async-start | bytes 589824 | tf_op jit(solution)/shard_map/reduce_scatter | solution.py:135
Sparse Core Ops, SparseCore 0:
  679.4 39.0 reduce-scatter.7
  722.1 38.5 reduce-scatter.3
  764.1 38.5 reduce-scatter.5
where the time goes:
time: 878 us; the launch traced here: 872 us
  blocking collectives  398 us (45%)
  waiting for transfers between devices  352 us (40%)
  matrix products  42.2 us (5%)
  local copies, waits for them, and re-layouts  35.9 us (4%)
  starting transfers between devices  26 us (3%)
  between operations  14 us (2%)
    all_to_all x1, blocking collectives, per_device(): lax.all_to_all(sent_rows, 'tile', split_axis=0, concat_axis=0, tiled=True)  204 us
    all_to_all x1, blocking collectives, per_device(): lax.all_to_all(scaled_sent, 'tile', split_axis=0, concat_axis=0, tiled=True)  194 us
    all_to_all x1, waiting for transfers between devices, per_device(): lax.all_to_all(partial_value.reshape(tile_count, count, D), 'tile', split...  180 us
    all_to_all x1, waiting for transfers between devices, per_device(): lax.all_to_all(tile_in.reshape(tile_count, -1, D), 'tile', split_axis=0,...  171 us
  transfers between devices with their start and end apart: 5, of which 2 were waited for; matrix products, arithmetic and copies ran while one was open for 2% of the time, Pallas kernels for 0%

commit v1 on v0

v1 whole, which is shorter than its diff:
```python
import jax
import jax.numpy as jnp
import numpy as np
from jax import lax
from jax.experimental import pallas as pl
from jax.experimental.pallas import tpu as pltpu
from jax.sharding import Mesh
from jax.sharding import PartitionSpec as P

D = 2048
TOPK = 8
TILE_W = 128
HTILES = 6
CAP = 10
NY, NC, NX = 4, 2, 4
D_PART = D // NY
UNITS = TILE_W // (NX * NC)
HALF = HTILES // 2 * UNITS
SOURCES = NX * NC
GROUP = NY * CAP
LANES = SOURCES * GROUP
VMEM_LIMIT = 48 * 1024 * 1024

CONTRACT_COLS = (((1,), (1,)), ((), ()))
CONTRACT_ROWS = (((0,), (0,)), ((), ()))


def shifted(value, axis, size, step):
    return lax.ppermute(value, axis, [(i, (i + step) % size) for i in range(size)])


def exchanged(value):
    return shifted(value, "c", NC, 1)


def swap(value, axis):
    return lax.all_to_all(value, axis, split_axis=0, concat_axis=0, tiled=True)


def whole(shape):
    return pl.BlockSpec(shape, lambda e, *_: (0,) * len(shape))


def slice_kernel(place, gate_ref, up_ref, down_ref, out_ref, turned):
    core = place[1]
    for matrix, ref in enumerate((gate_ref, up_ref, down_ref)):
        turned[...] = ref[0] if matrix == 2 else ref[0].T
        for x in range(NX):
            start = pl.multiple_of(x * NC * UNITS + core * UNITS, UNITS)
            out_ref[x, matrix * UNITS : (matrix + 1) * UNITS, :] = turned[pl.ds(start, UNITS), :]


def weight_slices(place, w_gate, w_up, w_down):
    return pl.pallas_call(
        slice_kernel,
        grid_spec=pltpu.PrefetchScalarGridSpec(
            num_scalar_prefetch=1,
            grid=(1,),
            in_specs=[
                pl.BlockSpec((1, D_PART, TILE_W), lambda i, place: (0, place[0], 0)),
                pl.BlockSpec((1, D_PART, TILE_W), lambda i, place: (0, place[0], 0)),
                pl.BlockSpec((1, TILE_W, D_PART), lambda i, place: (0, 0, place[0])),
            ],
            out_specs=whole((NX, 3 * UNITS, D_PART)),
            scratch_shapes=[pltpu.VMEM((TILE_W, D_PART), jnp.bfloat16)],
        ),
        out_shape=jax.ShapeDtypeStruct((NX, 3 * UNITS, D_PART), jnp.bfloat16),
        compiler_params=pltpu.CompilerParams(vmem_limit_bytes=VMEM_LIMIT),
    )(place, w_gate, w_up, w_down)


def expert_weight(slots, weights_ref, expert, matrix, tiles):
    rows = slice(matrix * UNITS, (matrix + 1) * UNITS)
    return [weights_ref[slots[expert * HTILES + h], rows, :] for h in tiles]


def both_rows(row_refs):
    blocks = [ref[0].astype(jnp.float32) for ref in row_refs]
    inputs = jnp.concatenate([b[:GROUP] for b in blocks], axis=0)
    scaled = jnp.concatenate([b[GROUP:] for b in blocks], axis=0)
    return inputs.astype(jnp.bfloat16), scaled.astype(jnp.bfloat16)


def partial_kernel(slots, weights_ref, *refs):
    row_refs, out_ref = refs[:SOURCES], refs[SOURCES]
    expert = pl.program_id(0)
    inputs, scaled = both_rows(row_refs)
    for matrix, rows in ((0, inputs), (1, inputs), (2, scaled)):
        weight = jnp.concatenate(
            expert_weight(slots, weights_ref, expert, matrix, range(HTILES)), axis=0
        )
        product = lax.dot_general(
            weight, rows, CONTRACT_COLS, preferred_element_type=jnp.float32
        ).astype(jnp.bfloat16)
        out_ref[0, matrix] = product[:HALF]
        out_ref[1, matrix] = product[HALF:]


def row_specs():
    return [pl.BlockSpec((1, 2 * GROUP, D_PART), lambda e, *_: (e, 0, 0))] * SOURCES


def partial_products(slots, weights, rows, experts):
    return pl.pallas_call(
        partial_kernel,
        grid_spec=pltpu.PrefetchScalarGridSpec(
            num_scalar_prefetch=1,
            grid=(experts,),
            in_specs=[whole(weights.shape)] + row_specs(),
            out_specs=pl.BlockSpec((2, 3, HALF, LANES), lambda e, *_: (e, 0, 0, 0)),
        ),
        out_shape=jax.ShapeDtypeStruct((2 * experts, 3, HALF, LANES), jnp.bfloat16),
        compiler_params=pltpu.CompilerParams(vmem_limit_bytes=VMEM_LIMIT),
    )(slots, weights, *rows)


def activation(act_ref, matrix):
    return jnp.concatenate([act_ref[0, matrix], act_ref[1, matrix]], axis=0)


def weight_grad_kernel(slots, act_ref, *refs):
    row_refs, out_ref = refs[:SOURCES], refs[SOURCES]
    expert = pl.program_id(0)

    @pl.when(expert == 0)
    def _():
        out_ref[...] = jnp.zeros_like(out_ref)

    inputs, scaled = both_rows(row_refs)
    for matrix, rows in ((0, inputs), (1, inputs), (2, scaled)):
        grad = jnp.dot(
            activation(act_ref, matrix), rows, preferred_element_type=jnp.float32
        ).astype(jnp.bfloat16)
        for h in range(HTILES):
            out_ref[slots[expert * HTILES + h], matrix * UNITS : (matrix + 1) * UNITS, :] = grad[
                h * UNITS : (h + 1) * UNITS
            ]


def act_spec():
    return pl.BlockSpec((2, 3, HALF, LANES), lambda e, *_: (e, 0, 0, 0))


def weight_grads(slots, acts, rows, experts, tile_count):
    shape = (tile_count, 3 * UNITS, D_PART)
    return pl.pallas_call(
        weight_grad_kernel,
        grid_spec=pltpu.PrefetchScalarGridSpec(
            num_scalar_prefetch=1,
            grid=(experts,),
            in_specs=[act_spec()] + row_specs(),
            out_specs=whole(shape),
        ),
        out_shape=jax.ShapeDtypeStruct(shape, jnp.bfloat16),
        compiler_params=pltpu.CompilerParams(vmem_limit_bytes=VMEM_LIMIT),
    )(slots, acts, *rows)


def output_kernel(slots, weights_ref, act_ref, *out_refs):
    expert = pl.program_id(0)
    tiles = range(HTILES)
    out = lax.dot_general(
        activation(act_ref, 2),
        jnp.concatenate(expert_weight(slots, weights_ref, expert, 2, tiles), axis=0),
        CONTRACT_ROWS,
        preferred_element_type=jnp.float32,
    )
    back = lax.dot_general(
        jnp.concatenate([activation(act_ref, 0), activation(act_ref, 1)], axis=0),
        jnp.concatenate(
            expert_weight(slots, weights_ref, expert, 0, tiles)
            + expert_weight(slots, weights_ref, expert, 1, tiles),
            axis=0,
        ),
        CONTRACT_ROWS,
        preferred_element_type=jnp.float32,
    )
    for b, ref in enumerate(out_refs):
        part = slice(b * GROUP, (b + 1) * GROUP)
        ref[0] = jnp.concatenate([out[part], back[part]], axis=0).astype(jnp.bfloat16)


def outputs(slots, weights, acts, experts):
    return pl.pallas_call(
        output_kernel,
        grid_spec=pltpu.PrefetchScalarGridSpec(
            num_scalar_prefetch=1,
            grid=(experts,),
            in_specs=[whole(weights.shape), act_spec()],
            out_specs=row_specs(),
        ),
        out_shape=[jax.ShapeDtypeStruct((experts, 2 * GROUP, D_PART), jnp.bfloat16)] * SOURCES,
        compiler_params=pltpu.CompilerParams(vmem_limit_bytes=VMEM_LIMIT),
    )(slots, weights, acts)


def regroup_matrix(experts, sent):
    e, kind, y, r = np.meshgrid(
        np.arange(experts), np.arange(2), np.arange(NY), np.arange(CAP), indexing="ij"
    )
    source = y * sent + kind * experts * CAP + e * CAP + r
    matrix = np.zeros((source.size, NY * sent), np.float32)
    matrix[np.arange(source.size), source.reshape(-1)] = 1
    return jnp.asarray(matrix, jnp.bfloat16)


def per_device(tokens, expert_ids, gates, tile_slot, w_gate, w_up, w_down, grad_out):
    z_count = lax.axis_size("z")
    tok_rows = tokens.shape[0]
    experts = tile_slot.shape[0] // HTILES
    slot_count = experts * CAP
    sent = -(-2 * slot_count // 16) * 16
    core = lax.axis_index("c")
    place = jnp.stack([lax.axis_index("y"), core]).astype(jnp.int32)
    slots = (tile_slot % z_count) * NX + tile_slot // z_count

    weight_parts = swap(weight_slices(place, w_gate, w_up, w_down), "x")
    weights = lax.all_gather(weight_parts, "z", axis=0, tiled=True)

    route_ids = expert_ids.reshape(-1)
    member = (route_ids[:, None] == jnp.arange(experts, dtype=jnp.int32)[None, :]).astype(jnp.int32)
    slot_rank = jnp.sum((jnp.cumsum(member, axis=0) - member) * member, axis=1)
    position = jnp.where(route_ids < experts, route_ids * CAP + slot_rank, slot_count)
    choose = (position[:, None] == jnp.arange(slot_count, dtype=jnp.int32)[None, :]).astype(
        jnp.float32
    )
    picker = jnp.sum(choose.reshape(tok_rows, TOPK, slot_count), axis=1)
    picker_half = picker.astype(jnp.bfloat16)
    gate_slot = jnp.dot(gates.reshape(-1), choose, precision=lax.Precision.HIGHEST)

    expert_rows = lax.dot_general(
        picker_half, tokens, CONTRACT_ROWS, preferred_element_type=jnp.float32
    ).astype(jnp.bfloat16)
    upstream = lax.dot_general(
        picker_half, grad_out, CONTRACT_ROWS, preferred_element_type=jnp.float32
    )
    scaled = (gate_slot[:, None] * upstream).astype(jnp.bfloat16)
    both = jnp.concatenate([expert_rows, scaled], axis=0)
    both = jnp.pad(both, ((0, sent - 2 * slot_count), (0, 0)))
    both = both.reshape(sent, NY, D_PART).transpose(1, 0, 2)
    regroup = regroup_matrix(experts, sent)
    own_rows = (
        jnp.dot(
            regroup,
            swap(both, "y").reshape(NY * sent, D_PART),
            preferred_element_type=jnp.float32,
        )
        .astype(jnp.bfloat16)
        .reshape(experts, 2 * GROUP, D_PART)
    )
    steps = (1, 3, 2)
    rows = [own_rows] + [shifted(own_rows, "x", NX, step) for step in steps]
    rows = rows + [exchanged(block) for block in rows]

    partial = swap(partial_products(slots, weights, rows, experts), "y")
    pieces = partial.shape[0] // NY
    total = jnp.sum(partial.reshape(NY, pieces, 3, HALF, LANES).astype(jnp.float32), axis=0)
    pre_gate, pre_up, hidden_grad = total[:, 0], total[:, 1], total[:, 2]
    sigmoid_gate = jax.nn.sigmoid(pre_gate)
    activated = pre_gate * sigmoid_gate
    acts = jnp.stack(
        [
            hidden_grad * pre_up * sigmoid_gate * (1.0 + pre_gate * (1.0 - sigmoid_gate)),
            hidden_grad * activated,
            activated * pre_up,
        ],
        axis=1,
    ).astype(jnp.bfloat16)
    acts = swap(jnp.tile(acts, (NY, 1, 1, 1)), "y")

    grads = weight_grads(slots, acts, rows, experts, z_count * NX)
    grads = lax.psum_scatter(grads, "z", scatter_dimension=0, tiled=True)
    grads = swap(grads, "x")
    half = D_PART // NC
    keep = lax.dynamic_slice_in_dim(grads, core * half, half, axis=2)
    give = lax.dynamic_slice_in_dim(grads, (1 - core) * half, half, axis=2)
    take = exchanged(give)
    pair = jnp.stack([jnp.where(core == 0, keep, take), jnp.where(core == 0, take, keep)], axis=1)
    pair = pair.reshape(NX, NC, 3, UNITS, half).transpose(2, 0, 1, 3, 4).reshape(3, TILE_W, half)
    gate_weight_grads = pair[0].T[None]
    up_weight_grads = pair[1].T[None]
    down_weight_grads = pair[2][None]

    blocks = outputs(slots, weights, acts, experts)
    far = [exchanged(block) for block in blocks[NX:]]
    near = [
        (a.astype(jnp.float32) + b.astype(jnp.float32)).astype(jnp.bfloat16)
        for a, b in zip(blocks[:NX], far, strict=True)
    ]
    home = near[0].astype(jnp.float32)
    for block, step in zip(near[1:], steps, strict=True):
        home = home + shifted(block, "x", NX, NX - step).astype(jnp.float32)
    home = lax.dot_general(
        regroup,
        home.astype(jnp.bfloat16).reshape(experts * 2 * GROUP, D_PART),
        CONTRACT_ROWS,
        preferred_element_type=jnp.float32,
    ).astype(jnp.bfloat16)
    home = swap(home.reshape(NY, sent, D_PART), "y").transpose(1, 0, 2).reshape(sent, D)
    expert_out = home[:slot_count].astype(jnp.float32)
    input_slot = home[slot_count : 2 * slot_count].astype(jnp.float32)
    layer_out = jnp.dot(
        picker, gate_slot[:, None] * expert_out, precision=lax.Precision.HIGHEST
    ).astype(jnp.bfloat16)
    gate_terms = jnp.sum(expert_out * upstream, axis=1)
    gate_grads = jnp.dot(choose, gate_terms, precision=lax.Precision.HIGHEST).reshape(
        tok_rows, TOPK
    )
    token_grads = jnp.dot(picker, input_slot, precision=lax.Precision.HIGHEST).astype(jnp.bfloat16)
    return (
        layer_out,
        token_grads,
        gate_grads,
        gate_weight_grads,
        up_weight_grads,
        down_weight_grads,
    )


def solution(mesh):
    dp, tile = ("y", "c"), ("x", "z")
    planes = Mesh(mesh.devices.reshape(NY, NC, NX, -1), dp + tile)
    rows = P(dp + tile, None)
    in_specs = (
        rows,
        rows,
        rows,
        P(),
        P(tile, None, None),
        P(tile, None, None),
        P(tile, None, None),
        rows,
    )
    out_specs = (
        rows,
        rows,
        rows,
        P(tile, dp, None),
        P(tile, dp, None),
        P(tile, None, dp),
    )
    return jax.shard_map(
        per_device, mesh=planes, in_specs=in_specs, out_specs=out_specs, check_vma=False
    )
```

time: 878 us -> 292 us (0.33)
  the two profiles are of different devices: /device:TPU:1 before, /device:TPU:321 now
where the time goes in v1:
time: 292 us; the launch traced here: 290 us
  blocking collectives  83.2 us (28%)
  starting transfers between devices  74.8 us (26%)
  waiting for transfers between devices  55.8 us (19%)
  Pallas kernels  30 us (10%)
  local copies, waits for them, and re-layouts  16.8 us (6%)
  between operations  14.6 us (5%)
  matrix products  8.95 us (3%)
  other arithmetic  5.86 us (2%)
    all_to_all x4, blocking collectives, swap(): return lax.all_to_all(value, axis, split_axis=0, concat_axis=0, tiled=True)  83.2 us
    ppermute x15, starting transfers between devices, shifted(): lax.ppermute(value, axis, [(i, (i + step) % size) for i in range(size)])  67.6 us
    ppermute x15, waiting for transfers between devices, shifted(): lax.ppermute(value, axis, [(i, (i + step) % size) for i in range(size)])  39.8 us
    all_to_all x2, waiting for transfers between devices, swap(): return lax.all_to_all(value, axis, split_axis=0, concat_axis=0, tiled=True)  16 us
    unnamed x48, local copies, waits for them, and re-layouts  14.5 us
    pallas_call x1, Pallas kernels, partial_products(): pl.pallas_call(partial_kernel, grid_spec=pltpu.PrefetchScalarGridSpec(num...  9.99 us
    pallas_call x1, Pallas kernels, weight_grads(): pl.pallas_call(weight_grad_kernel, grid_spec=pltpu.PrefetchScalarGridSpec...  9.69 us
    pallas_call x1, Pallas kernels, outputs(): pl.pallas_call(output_kernel, grid_spec=pltpu.PrefetchScalarGridSpec(num_...  9.64 us
  transfers between devices with their start and end apart: 19, of which 6 were waited for; matrix products, arithmetic and copies ran while one was open for 6% of the time, Pallas kernels for 3%

profile of v1, /device:TPU:321, one launch (start us, length us, event | category | flops | bytes accessed | tf_op | source)
XLA Modules:
  0.0 290.0 jit_solution(17290931096672371029)
XLA Ops:
  11.1 9.1 %all_to_all.30 = bf16[4,48,512]{2,1,0:T(8,128)(2,1)} all-to-all(bf16[4,48,512]{2,1,0:T(8,128)(2,1)S(1)} %shard_map.136), channel_id=1, replica_groups=mesh['y'=4,'c'=2,'x'=4,'z'=16] {'x'}, dimensions={0} | all-to-all | bytes 393216 | tf_op jit(solution)/shard_map/all_to_all | solution.py:37
  20.6 2.8 reduce-window.6
  26.6 14.5 %all_to_all.31 = bf16[4,208,512]{2,1,0:T(8,128)(2,1)S(1)} all-to-all(bf16[4,208,512]{2,1,0:T(8,128)(2,1)S(1)} %bitcast.83), channel_id=1, replica_groups=mesh['y'=4,'c'=2,'x'=4,'z'=16] {'y'}, dimensions={0} | all-to-all | bytes 1703936 | tf_op jit(solution)/shard_map/all_to_all | solution.py:37
  42.0 2.7 collective-permute-start
  44.8 3.8 %collective-permute-start.1 = (bf16[10,80,512]{2,1,0:T(8,128)(2,1)S(1)}, bf16[10,80,512]{2,1,0:T(8,128)(2,1)S(1)}, u32[]{:S(2)}, u32[]{:S(2)}) collective-permute-start(bf16[10,80,512]{2,1,0:T(8,128)(2,1)S(1)} %bitcast.71), channel_id=1, source_target_pairs={{0,48},{16,0},{32,16},{48,32},{1,49},{17,1},{33,17},{49,33},{2,50}... | collective-permute-start | bytes 2457608 | tf_op jit(solution)/shard_map/ppermute | solution.py:29
  50.9 5.8 %collective-permute-start.3 = (bf16[10,80,512]{2,1,0:T(8,128)(2,1)S(1)}, bf16[10,80,512]{2,1,0:T(8,128)(2,1)S(1)}, u32[]{:S(2)}, u32[]{:S(2)}) collective-permute-start(bf16[10,80,512]{2,1,0:T(8,128)(2,1)S(1)} %bitcast.73), channel_id=1, source_target_pairs={{0,64},{64,0},{1,65},{65,1},{2,66},{66,2},{3,67},{67,3},{4,68},{68... | collective-permute-start | bytes 2457608 | tf_op jit(solution)/shard_map/ppermute | solution.py:29
  56.6 5.3 %collective-permute-done.refs_1_ = bf16[10,80,512]{2,1,0:T(8,128)(2,1)S(1)} collective-permute-done((bf16[10,80,512]{2,1,0:T(8,128)(2,1)S(1)}, bf16[10,80,512]{2,1,0:T(8,128)(2,1)S(1)}, u32[]{:S(2)}, u32[]{:S(2)}) %collective-permute-start) | collective-permute-done | bytes 819232 | tf_op jit(solution)/shard_map/ppermute | solution.py:29
  61.9 23.4 %collective-permute-start.4 = (bf16[10,80,512]{2,1,0:T(8,128)(2,1)S(1)}, bf16[10,80,512]{2,1,0:T(8,128)(2,1)S(1)}, u32[]{:S(2)}, u32[]{:S(2)}) collective-permute-start(bf16[10,80,512]{2,1,0:T(8,128)(2,1)S(1)} %collective-permute-done.refs_1_), channel_id=1, source_target_pairs={{0,64},{64,0},{1,65},{65,1},{2,66},{66,2},{3,67},{67,3},{4,68},{68... | collective-permute-start | bytes 2457608 | tf_op jit(solution)/shard_map/ppermute | solution.py:29
  87.2 2.4 collective-permute-start.6
  97.9 10.0 %shard_map.137 = bf16[20,3,48,320]{3,2,1,0:T(8,128)(2,1)} custom-call(s32[60]{0:T(128)S(1)} %fusion.15.slots, bf16[64,48,512]{2,1,0:T(8,128)(2,1)} %all-gather.2.cloned.1.call-done.weights_ref, bf16[10,80,512]{2,1,0:T(8,128)(2,1)S(1)} %bitcast.74, bf16[10,80,512]{2,1,0:T(8,128)(2,1)S(1)} %collective-permute-done.refs_1_, ...), custom_call_target="tpu_custom_call" | custom-call | tf_op jit(solution)/shard_map/pallas_call | solution.py:104
  107.9 30.4 %all_to_all.32 = bf16[20,3,48,320]{3,2,1,0:T(8,128)(2,1)S(1)} all-to-all(bf16[20,3,48,320]{3,2,1,0:T(8,128)(2,1)} %shard_map.137), channel_id=1, replica_groups=mesh['y'=4,'c'=2,'x'=4,'z'=16] {'y'}, dimensions={0} | all-to-all | bytes 3686400 | tf_op jit(solution)/shard_map/all_to_all | solution.py:37
  139.3 29.2 %all_to_all.33.act_ref = bf16[20,3,48,320]{3,2,1,0:T(8,128)(2,1)} all-to-all(bf16[20,3,48,320]{3,2,1,0:T(8,128)(2,1)S(1)} %bitcast.77), channel_id=1, replica_groups=mesh['y'=4,'c'=2,'x'=4,'z'=16] {'y'}, dimensions={0} | all-to-all | bytes 3686400 | tf_op jit(solution)/shard_map/all_to_all | solution.py:37
  168.4 9.7 %shard_map.139 = bf16[64,48,512]{2,1,0:T(8,128)(2,1)} custom-call(s32[60]{0:T(128)S(1)} %fusion.15.slots, bf16[20,3,48,320]{3,2,1,0:T(8,128)(2,1)} %all_to_all.33.act_ref, bf16[10,80,512]{2,1,0:T(8,128)(2,1)S(1)} %bitcast.75, bf16[10,80,512]{2,1,0:T(8,128)(2,1)S(1)} %collective-permute-done.refs_1_, bf16[10,80,512]{2,1,0:T(8,128)(2,1)S(1)} %collective-permute-done.1.refs_2_, ...), custom_call_target="tpu_custom_call" | custom-call | tf_op jit(solution)/shard_map/pallas_call | solution.py:146
  178.2 9.6 %shard_map.138 = (bf16[10,80,512]{2,1,0:T(8,128)(2,1)S(1)}, bf16[10,80,512]{2,1,0:T(8,128)(2,1)S(1)}, bf16[10,80,512]{2,1,0:T(8,128)(2,1)S(1)}, bf16[10,80,512]{...) custom-call(s32[60]{0:T(128)S(1)} %fusion.15.slots, ...), custom_call_target="tpu_custom_call" | custom-call | tf_op jit(solution)/shard_map/pallas_call | solution.py:184
  187.8 4.5 %collective-permute-start.8 = (bf16[10,80,512]{2,1,0:T(8,128)(2,1)S(1)}, bf16[10,80,512]{2,1,0:T(8,128)(2,1)S(1)}, u32[]{:S(2)}, u32[]{:S(2)}) collective-permute-start(bf16[10,80,512]{2,1,0:T(8,128)(2,1)S(1)} %get-tuple-element.17), channel_id=1, source_target_pairs={{0,64},{64,0},{1,65},{65,1},{2,66},{66,2},{3,67},{67,3},{4,68},{68... | collective-permute-start | bytes 2457608 | tf_op jit(solution)/shard_map/ppermute | solution.py:29
  198.8 4.0 %collective-permute-start.9 = (bf16[10,80,512]{2,1,0:T(8,128)(2,1)S(1)}, bf16[10,80,512]{2,1,0:T(8,128)(2,1)S(1)}, u32[]{:S(2)}, u32[]{:S(2)}) collective-permute-start(bf16[10,80,512]{2,1,0:T(8,128)(2,1)S(1)} %add_convert_fusion.3), channel_id=1, source_target_pairs={{0,48},{16,0},{32,16},{48,32},{1,49},{17,1},{33,17},{49,33},{2,50}... | collective-permute-start | bytes 2457608 | tf_op jit(solution)/shard_map/ppermute | solution.py:29
  205.2 3.1 %collective-permute-start.13 = (bf16[10,80,512]{2,1,0:T(8,128)(2,1)S(1)}, bf16[10,80,512]{2,1,0:T(8,128)(2,1)S(1)}, u32[]{:S(2)}, u32[]{:S(2)}) collective-permute-start(bf16[10,80,512]{2,1,0:T(8,128)(2,1)S(1)} %add_convert_fusion.1), channel_id=1, source_target_pairs={{0,32},{16,48},{32,0},{48,16},{1,33},{17,49},{33,1},{49,17},{2,34}... | collective-permute-start | bytes 2457608 | tf_op jit(solution)/shard_map/ppermute | solution.py:29
  208.4 11.9 %collective-permute-done.9 = bf16[10,80,512]{2,1,0:T(8,128)(2,1)S(1)} collective-permute-done((bf16[10,80,512]{2,1,0:T(8,128)(2,1)S(1)}, bf16[10,80,512]{2,1,0:T(8,128)(2,1)S(1)}, u32[]{:S(2)}, u32[]{:S(2)}) %collective-permute-start.9) | collective-permute-done | bytes 819232 | tf_op jit(solution)/shard_map/ppermute | solution.py:29
  220.3 22.4 %collective-permute-done.11 = bf16[10,80,512]{2,1,0:T(8,128)(2,1)S(1)} collective-permute-done((bf16[10,80,512]{2,1,0:T(8,128)(2,1)S(1)}, bf16[10,80,512]{2,1,0:T(8,128)(2,1)S(1)}, u32[]{:S(2)}, u32[]{:S(2)}) %collective-permute-start.11) | collective-permute-done | bytes 819232 | tf_op jit(solution)/shard_map/ppermute | solution.py:29
  246.1 3.7 %all-to-all-start.4 = ((bf16[4,208,512]{2,1,0:T(8,128)(2,1)}), bf16[4,208,512]{2,1,0:T(8,128)(2,1)S(1)}, u32[]{:S(2)}, u32[]{:S(2)}) async-start(bf16[4,208,512]{2,1,0:T(8,128)(2,1)} %bitcast.14), calls=%async_computation.4 | async-start | bytes 1703936 | tf_op jit(solution)/shard_map/all_to_all | solution.py:37
  249.8 11.1 %all-to-all-done.4 = bf16[4,208,512]{2,1,0:T(8,128)(2,1)S(1)} async-done(((bf16[4,208,512]{2,1,0:T(8,128)(2,1)}), bf16[4,208,512]{2,1,0:T(8,128)(2,1)S(1)}, u32[]{:S(2)}, u32[]{:S(2)}) %all-to-all-start.4) | async-done | bytes 852000 | tf_op jit(solution)/shard_map/all_to_all | solution.py:37
  265.8 3.4 %all-to-all-start.5 = ((bf16[4,48,512]{2,1,0:T(8,128)(2,1)}), bf16[4,48,512]{2,1,0:T(8,128)(2,1)S(1)}, u32[]{:S(2)}, u32[]{:S(2)}) async-start(bf16[4,48,512]{2,1,0:T(8,128)(2,1)} %reduce-scatter.2.cloned.1.call-done), calls=%async_computation.6 | async-start | bytes 393216 | tf_op jit(solution)/shard_map/all_to_all | solution.py:37
  269.4 5.0 %all-to-all-done.5 = bf16[4,48,512]{2,1,0:T(8,128)(2,1)S(1)} async-done(((bf16[4,48,512]{2,1,0:T(8,128)(2,1)}), bf16[4,48,512]{2,1,0:T(8,128)(2,1)S(1)}, u32[]{:S(2)}, u32[]{:S(2)}) %all-to-all-start.5) | async-done | bytes 196640 | tf_op jit(solution)/shard_map/all_to_all | solution.py:37
  274.3 5.6 %collective-permute-start.14 = (bf16[4,48,256]{2,1,0:T(8,128)(2,1)S(1)}, bf16[4,48,256]{2,1,0:T(8,128)(2,1)S(1)}, u32[]{:S(2)}, u32[]{:S(2)}) collective-permute-start(bf16[4,48,256]{2,1,0:T(8,128)(2,1)S(1)} %constant_dynamic-slice_fusion), channel_id=1, source_target_pairs={{0,64},{64,0},{1,65},{65,1},{2,66},{66,2},{3,67},{67,3},{4,68},{68... | collective-permute-start | bytes 294920 | tf_op jit(solution)/shard_map/ppermute | solution.py:29
  (118 shorter events, 42.1 us)
Async XLA Ops:
  7.2 18.0 %copy-start = (bf16[128,2048]{1,0:T(8,128)(2,1)S(1)}, bf16[128,2048]{1,0:T(8,128)(2,1)}, u32[]{:S(2)}) copy-start(bf16[128,2048]{1,0:T(8,128)(2,1)} %param.16) | copy-start | bytes 1572868
  7.2 86.1 %all-gather.2.cloned.1.call-start = ((), (), s32[]{:S(2)}) async-start(), calls=%async_computation.7 | async-start | bytes 3342336 | tf_op jit(solution)/shard_map/all_gather | solution.py:218
  10.4 13.6 %copy-start.15 = (f32[128,8]{0,1:T(8,128)S(1)}, f32[128,8]{0,1:T(8,128)}, u32[]{:S(2)}) copy-start(f32[128,8]{0,1:T(8,128)} %param.11) | copy-start | bytes 12292
  10.4 14.4 %copy-start.13 = (bf16[128,2048]{1,0:T(8,128)(2,1)S(1)}, bf16[128,2048]{1,0:T(8,128)(2,1)}, u32[]{:S(2)}) copy-start(bf16[128,2048]{1,0:T(8,128)(2,1)} %param.9) | copy-start | bytes 1572868
  20.3 245.6 %reduce-scatter.2.cloned.1.call-start = ((), (), s32[]{:S(2)}) async-start(), calls=%async_computation.8 | async-start | bytes 3342336 | tf_op jit(solution)/shard_map/reduce_scatter | solution.py:272
  26.5 14.5 %copy-start.17 = (bf16[800,832]{1,0:T(8,128)(2,1)S(1)}, bf16[800,832]{1,0:T(8,128)(2,1)}, u32[]{:S(2)}) copy-start(bf16[800,832]{1,0:T(8,128)(2,1)} %constant.63.clone) | copy-start | bytes 3993604
  41.0 49.5 %copy-start.16 = (s32[60]{0:T(128)S(1)}, s32[60]{0:T(128)}, u32[]{:S(2)}) copy-start(s32[60]{0:T(128)} %param.12) | copy-start | bytes 724
  42.0 19.8 %collective-permute-start = (bf16[10,80,512]{2,1,0:T(8,128)(2,1)S(1)}, bf16[10,80,512]{2,1,0:T(8,128)(2,1)S(1)}, u32[]{:S(2)}, u32[]{:S(2)}) collective-permute-start(bf16[10,80,512]{2,1,0:T(8,128)(2,1)S(1)} %bitcast.70), channel_id=1, source_target_pairs={{0,16},{16,32},{32,48},{48,0},{1,17},{17,33},{33,49},{49,1},{2,18}... | collective-permute-start | bytes 2457608 | tf_op jit(solution)/shard_map/ppermute | solution.py:29
  44.8 40.5 %collective-permute-start.1 = (bf16[10,80,512]{2,1,0:T(8,128)(2,1)S(1)}, bf16[10,80,512]{2,1,0:T(8,128)(2,1)S(1)}, u32[]{:S(2)}, u32[]{:S(2)}) collective-permute-start(bf16[10,80,512]{2,1,0:T(8,128)(2,1)S(1)} %bitcast.71), channel_id=1, source_target_pairs={{0,48},{16,0},{32,16},{48,32},{1,49},{17,1},{33,17},{49,33},{2,50}... | collective-permute-start | bytes 2457608 | tf_op jit(solution)/shard_map/ppermute | solution.py:29
  48.6 38.7 %collective-permute-start.2 = (bf16[10,80,512]{2,1,0:T(8,128)(2,1)S(1)}, bf16[10,80,512]{2,1,0:T(8,128)(2,1)S(1)}, u32[]{:S(2)}, u32[]{:S(2)}) collective-permute-start(bf16[10,80,512]{2,1,0:T(8,128)(2,1)S(1)} %bitcast.72), channel_id=1, source_target_pairs={{0,32},{16,48},{32,0},{48,16},{1,33},{17,49},{33,1},{49,17},{2,34}... | collective-permute-start | bytes 2457608 | tf_op jit(solution)/shard_map/ppermute | solution.py:29
  50.9 39.7 %collective-permute-start.3 = (bf16[10,80,512]{2,1,0:T(8,128)(2,1)S(1)}, bf16[10,80,512]{2,1,0:T(8,128)(2,1)S(1)}, u32[]{:S(2)}, u32[]{:S(2)}) collective-permute-start(bf16[10,80,512]{2,1,0:T(8,128)(2,1)S(1)} %bitcast.73), channel_id=1, source_target_pairs={{0,64},{64,0},{1,65},{65,1},{2,66},{66,2},{3,67},{67,3},{4,68},{68... | collective-permute-start | bytes 2457608 | tf_op jit(solution)/shard_map/ppermute | solution.py:29
  61.9 29.6 %collective-permute-start.4 = (bf16[10,80,512]{2,1,0:T(8,128)(2,1)S(1)}, bf16[10,80,512]{2,1,0:T(8,128)(2,1)S(1)}, u32[]{:S(2)}, u32[]{:S(2)}) collective-permute-start(bf16[10,80,512]{2,1,0:T(8,128)(2,1)S(1)} %collective-permute-done.refs_1_), channel_id=1, source_target_pairs={{0,64},{64,0},{1,65},{65,1},{2,66},{66,2},{3,67},{67,3},{4,68},{68... | collective-permute-start | bytes 2457608 | tf_op jit(solution)/shard_map/ppermute | solution.py:29
  85.3 7.1 %collective-permute-start.5 = (bf16[10,80,512]{2,1,0:T(8,128)(2,1)S(1)}, bf16[10,80,512]{2,1,0:T(8,128)(2,1)S(1)}, u32[]{:S(2)}, u32[]{:S(2)}) collective-permute-start(bf16[10,80,512]{2,1,0:T(8,128)(2,1)S(1)} %collective-permute-done.1.refs_2_), channel_id=1, source_target_pairs={{0,64},{64,0},{1,65},{65,1},{2,66},{66,2},{3,67},{67,3},{4,68},{68... | collective-permute-start | bytes 2457608 | tf_op jit(solution)/shard_map/ppermute | solution.py:29
  87.2 6.1 %collective-permute-start.6 = (bf16[10,80,512]{2,1,0:T(8,128)(2,1)S(1)}, bf16[10,80,512]{2,1,0:T(8,128)(2,1)}, u32[]{:S(2)}, u32[]{:S(2)}) collective-permute-start(bf16[10,80,512]{2,1,0:T(8,128)(2,1)S(1)} %collective-permute-done.2.refs_3_), channel_id=1, source_target_pairs={{0,64},{64,0},{1,65},{65,1},{2,66},{66,2},{3,67},{67,3},{4,68},{68... | collective-permute-start | bytes 2457608 | tf_op jit(solution)/shard_map/ppermute | solution.py:29
  187.8 10.8 %collective-permute-start.8 = (bf16[10,80,512]{2,1,0:T(8,128)(2,1)S(1)}, bf16[10,80,512]{2,1,0:T(8,128)(2,1)S(1)}, u32[]{:S(2)}, u32[]{:S(2)}) collective-permute-start(bf16[10,80,512]{2,1,0:T(8,128)(2,1)S(1)} %get-tuple-element.17), channel_id=1, source_target_pairs={{0,64},{64,0},{1,65},{65,1},{2,66},{66,2},{3,67},{67,3},{4,68},{68... | collective-permute-start | bytes 2457608 | tf_op jit(solution)/shard_map/ppermute | solution.py:29
  192.3 10.5 %collective-permute-start.10 = (bf16[10,80,512]{2,1,0:T(8,128)(2,1)S(1)}, bf16[10,80,512]{2,1,0:T(8,128)(2,1)S(1)}, u32[]{:S(2)}, u32[]{:S(2)}) collective-permute-start(bf16[10,80,512]{2,1,0:T(8,128)(2,1)S(1)} %get-tuple-element.19), channel_id=1, source_target_pairs={{0,64},{64,0},{1,65},{65,1},{2,66},{66,2},{3,67},{67,3},{4,68},{68... | collective-permute-start | bytes 2457608 | tf_op jit(solution)/shard_map/ppermute | solution.py:29
  194.2 10.8 %collective-permute-start.12 = (bf16[10,80,512]{2,1,0:T(8,128)(2,1)}, bf16[10,80,512]{2,1,0:T(8,128)(2,1)S(1)}, u32[]{:S(2)}, u32[]{:S(2)}) collective-permute-start(bf16[10,80,512]{2,1,0:T(8,128)(2,1)} %get-tuple-element.21), channel_id=1, source_target_pairs={{0,64},{64,0},{1,65},{65,1},{2,66},{66,2},{3,67},{67,3},{4,68},{68... | collective-permute-start | bytes 2457608 | tf_op jit(solution)/shard_map/ppermute | solution.py:29
  196.6 11.7 %collective-permute-start.7 = (bf16[10,80,512]{2,1,0:T(8,128)(2,1)S(1)}, bf16[10,80,512]{2,1,0:T(8,128)(2,1)S(1)}, u32[]{:S(2)}, u32[]{:S(2)}) collective-permute-start(bf16[10,80,512]{2,1,0:T(8,128)(2,1)S(1)} %get-tuple-element.15), channel_id=1, source_target_pairs={{0,64},{64,0},{1,65},{65,1},{2,66},{66,2},{3,67},{67,3},{4,68},{68... | collective-permute-start | bytes 2457608 | tf_op jit(solution)/shard_map/ppermute | solution.py:29
  198.8 21.5 %collective-permute-start.9 = (bf16[10,80,512]{2,1,0:T(8,128)(2,1)S(1)}, bf16[10,80,512]{2,1,0:T(8,128)(2,1)S(1)}, u32[]{:S(2)}, u32[]{:S(2)}) collective-permute-start(bf16[10,80,512]{2,1,0:T(8,128)(2,1)S(1)} %add_convert_fusion.3), channel_id=1, source_target_pairs={{0,48},{16,0},{32,16},{48,32},{1,49},{17,1},{33,17},{49,33},{2,50}... | collective-permute-start | bytes 2457608 | tf_op jit(solution)/shard_map/ppermute | solution.py:29
  203.1 39.7 %collective-permute-start.11 = (bf16[10,80,512]{2,1,0:T(8,128)(2,1)S(1)}, bf16[10,80,512]{2,1,0:T(8,128)(2,1)S(1)}, u32[]{:S(2)}, u32[]{:S(2)}) collective-permute-start(bf16[10,80,512]{2,1,0:T(8,128)(2,1)S(1)} %add_convert_fusion.2), channel_id=1, source_target_pairs={{0,16},{16,32},{32,48},{48,0},{1,17},{17,33},{33,49},{49,1},{2,18}... | collective-permute-start | bytes 2457608 | tf_op jit(solution)/shard_map/ppermute | solution.py:29
  205.2 37.5 %collective-permute-start.13 = (bf16[10,80,512]{2,1,0:T(8,128)(2,1)S(1)}, bf16[10,80,512]{2,1,0:T(8,128)(2,1)S(1)}, u32[]{:S(2)}, u32[]{:S(2)}) collective-permute-start(bf16[10,80,512]{2,1,0:T(8,128)(2,1)S(1)} %add_convert_fusion.1), channel_id=1, source_target_pairs={{0,32},{16,48},{32,0},{48,16},{1,33},{17,49},{33,1},{49,17},{2,34}... | collective-permute-start | bytes 2457608 | tf_op jit(solution)/shard_map/ppermute | solution.py:29
  246.1 14.8 %all-to-all-start.4 = ((bf16[4,208,512]{2,1,0:T(8,128)(2,1)}), bf16[4,208,512]{2,1,0:T(8,128)(2,1)S(1)}, u32[]{:S(2)}, u32[]{:S(2)}) async-start(bf16[4,208,512]{2,1,0:T(8,128)(2,1)} %bitcast.14), calls=%async_computation.4 | async-start | bytes 1703936 | tf_op jit(solution)/shard_map/all_to_all | solution.py:37
  265.8 8.5 %all-to-all-start.5 = ((bf16[4,48,512]{2,1,0:T(8,128)(2,1)}), bf16[4,48,512]{2,1,0:T(8,128)(2,1)S(1)}, u32[]{:S(2)}, u32[]{:S(2)}) async-start(bf16[4,48,512]{2,1,0:T(8,128)(2,1)} %reduce-scatter.2.cloned.1.call-done), calls=%async_computation.6 | async-start | bytes 393216 | tf_op jit(solution)/shard_map/all_to_all | solution.py:37
  274.3 6.6 %collective-permute-start.14 = (bf16[4,48,256]{2,1,0:T(8,128)(2,1)S(1)}, bf16[4,48,256]{2,1,0:T(8,128)(2,1)S(1)}, u32[]{:S(2)}, u32[]{:S(2)}) collective-permute-start(bf16[4,48,256]{2,1,0:T(8,128)(2,1)S(1)} %constant_dynamic-slice_fusion), channel_id=1, source_target_pairs={{0,64},{64,0},{1,65},{65,1},{2,66},{66,2},{3,67},{67,3},{4,68},{68... | collective-permute-start | bytes 294920 | tf_op jit(solution)/shard_map/ppermute | solution.py:29
  (14 other events, 32.6 us)
Sparse Core Ops, SparseCore 0:
  20.4 63.9 all-gather.1
  178.3 63.4 reduce-scatter.1

commit v2 on v1

v2 whole, which is shorter than its diff:
```python
import jax
import jax.numpy as jnp
import numpy as np
from jax import lax
from jax.experimental import pallas as pl
from jax.experimental.pallas import tpu as pltpu
from jax.sharding import Mesh
from jax.sharding import PartitionSpec as P

D = 2048
TOPK = 8
TILE_W = 128
HTILES = 6
CAP = 10
NY, NC, NX = 4, 2, 4
D_PART = D // NY
UNITS = TILE_W // (NX * NC)
HALF = HTILES // 2 * UNITS
SOURCES = NX * NC
GROUP = NY * CAP
LANES = SOURCES * GROUP
PACKED = HALF * LANES // 128
STEP = 2
VMEM_LIMIT = 48 * 1024 * 1024

CONTRACT_COLS = (((1,), (1,)), ((), ()))
CONTRACT_ROWS = (((0,), (0,)), ((), ()))


def shifted(value, axis, size, step):
    return lax.ppermute(value, axis, [(i, (i + step) % size) for i in range(size)])


def exchanged(value):
    return shifted(value, "c", NC, 1)


def swap(value, axis):
    return lax.all_to_all(value, axis, split_axis=0, concat_axis=0, tiled=True)


def whole(shape):
    return pl.BlockSpec(shape, lambda e, *_: (0,) * len(shape))


def slice_kernel(gate_ref, up_ref, down_ref, out_ref, gate, up, down, turned, sems):
    core = lax.axis_index("c")
    part = pl.ds(pl.multiple_of(lax.axis_index("y") * D_PART, D_PART), D_PART)
    copies = [
        pltpu.make_async_copy(gate_ref.at[0, part, :], gate, sems.at[0]),
        pltpu.make_async_copy(up_ref.at[0, part, :], up, sems.at[1]),
        pltpu.make_async_copy(down_ref.at[0, :, part], down, sems.at[2]),
    ]
    for copy in copies:
        copy.start()
    for matrix, (copy, part_ref) in enumerate(zip(copies, (gate, up, down), strict=True)):
        copy.wait()
        if matrix < 2:
            turned[...] = part_ref[...].T
            part_ref = turned
        for x in range(NX):
            start = pl.multiple_of(x * NC * UNITS + core * UNITS, UNITS)
            out_ref[x, matrix * UNITS : (matrix + 1) * UNITS, :] = part_ref[pl.ds(start, UNITS), :]


def weight_slices(w_gate, w_up, w_down):
    return pl.pallas_call(
        slice_kernel,
        in_specs=[pl.BlockSpec(memory_space=pltpu.HBM)] * 3,
        out_shape=jax.ShapeDtypeStruct((NX, 3 * UNITS, D_PART), jnp.bfloat16),
        scratch_shapes=[
            pltpu.VMEM((D_PART, TILE_W), jnp.bfloat16),
            pltpu.VMEM((D_PART, TILE_W), jnp.bfloat16),
            pltpu.VMEM((TILE_W, D_PART), jnp.bfloat16),
            pltpu.VMEM((TILE_W, D_PART), jnp.bfloat16),
            pltpu.SemaphoreType.DMA((3,)),
        ],
        compiler_params=pltpu.CompilerParams(vmem_limit_bytes=VMEM_LIMIT),
    )(w_gate, w_up, w_down)


def parted_kernel(*refs):
    row_refs, (inputs_ref, scaled_ref) = refs[:NX], refs[NX:]
    blocks = [ref[...].astype(jnp.float32) for ref in row_refs]
    inputs_ref[...] = jnp.concatenate([b[:, :GROUP] for b in blocks], axis=1).astype(jnp.bfloat16)
    scaled_ref[...] = jnp.concatenate([b[:, GROUP:] for b in blocks], axis=1).astype(jnp.bfloat16)


def parted_rows(blocks, experts):
    return pl.pallas_call(
        parted_kernel,
        grid=(experts // STEP,),
        in_specs=[expert_spec(2 * GROUP)] * NX,
        out_specs=[expert_spec(NX * GROUP)] * 2,
        out_shape=[jax.ShapeDtypeStruct((experts, NX * GROUP, D_PART), jnp.bfloat16)] * 2,
        compiler_params=pltpu.CompilerParams(vmem_limit_bytes=VMEM_LIMIT),
    )(*blocks)


def expert_spec(rows):
    return pl.BlockSpec((STEP, rows, D_PART), lambda e, *_: (e, 0, 0))


def piece_spec():
    return pl.BlockSpec((2 * STEP, 3 * PACKED, 128), lambda e, *_: (e, 0, 0))


def expert_weight(slots, weights_ref, expert, matrix):
    rows = slice(matrix * UNITS, (matrix + 1) * UNITS)
    return jnp.concatenate(
        [weights_ref[slots[expert * HTILES + h], rows, :] for h in range(HTILES)], axis=0
    )


def packed(values):
    mid = HALF // 2
    rest = jnp.concatenate([values[:mid, 256:], values[mid:, 256:]], axis=1)
    return jnp.concatenate([values[:, :128], values[:, 128:256], rest], axis=0)


def unpacked(values):
    rest = values[2 * HALF :]
    rest = jnp.concatenate([rest[:, :64], rest[:, 64:]], axis=0)
    return jnp.concatenate([values[:HALF], values[HALF : 2 * HALF], rest], axis=1)


def partial_kernel(slots, weights_ref, *refs):
    near_inputs, near_scaled, far_inputs, far_scaled, out_ref = refs
    for i in range(STEP):
        expert = pl.program_id(0) * STEP + i
        inputs = jnp.concatenate([near_inputs[i], far_inputs[i]], axis=0)
        scaled = jnp.concatenate([near_scaled[i], far_scaled[i]], axis=0)
        products = [
            lax.dot_general(
                expert_weight(slots, weights_ref, expert, matrix),
                rows,
                CONTRACT_COLS,
                preferred_element_type=jnp.float32,
            )
            for matrix, rows in ((0, inputs), (1, inputs), (2, scaled))
        ]
        for half in range(2):
            part = slice(half * HALF, (half + 1) * HALF)
            out_ref[2 * i + half] = jnp.concatenate(
                [packed(p[part]) for p in products], axis=0
            ).astype(jnp.bfloat16)


def partial_products(slots, weights, rows, experts):
    return pl.pallas_call(
        partial_kernel,
        grid_spec=pltpu.PrefetchScalarGridSpec(
            num_scalar_prefetch=1,
            grid=(experts // STEP,),
            in_specs=[whole(weights.shape)] + [expert_spec(NX * GROUP)] * 4,
            out_specs=piece_spec(),
        ),
        out_shape=jax.ShapeDtypeStruct((2 * experts, 3 * PACKED, 128), jnp.bfloat16),
        compiler_params=pltpu.CompilerParams(vmem_limit_bytes=VMEM_LIMIT),
    )(slots, weights, *rows)


def activations(act_ref, i):
    pieces = [act_ref[2 * i + half].astype(jnp.float32) for half in range(2)]
    return [
        jnp.concatenate(
            [unpacked(p[matrix * PACKED : (matrix + 1) * PACKED]) for p in pieces], axis=0
        ).astype(jnp.bfloat16)
        for matrix in range(3)
    ]


def weight_grad_kernel(slots, act_ref, *refs):
    near_inputs, near_scaled, far_inputs, far_scaled, out_ref = refs

    @pl.when(pl.program_id(0) == 0)
    def _():
        out_ref[...] = jnp.zeros_like(out_ref)

    for i in range(STEP):
        expert = pl.program_id(0) * STEP + i
        inputs = jnp.concatenate([near_inputs[i], far_inputs[i]], axis=0)
        scaled = jnp.concatenate([near_scaled[i], far_scaled[i]], axis=0)
        acts = activations(act_ref, i)
        for matrix, rows in enumerate((inputs, inputs, scaled)):
            grad = jnp.dot(acts[matrix], rows, preferred_element_type=jnp.float32)
            grad = grad.astype(jnp.bfloat16)
            for h in range(HTILES):
                slot = slots[expert * HTILES + h]
                out_ref[slot, matrix * UNITS : (matrix + 1) * UNITS, :] = grad[
                    h * UNITS : (h + 1) * UNITS
                ]


def weight_grads(slots, acts, rows, experts, tile_count):
    shape = (tile_count, 3 * UNITS, D_PART)
    return pl.pallas_call(
        weight_grad_kernel,
        grid_spec=pltpu.PrefetchScalarGridSpec(
            num_scalar_prefetch=1,
            grid=(experts // STEP,),
            in_specs=[piece_spec()] + [expert_spec(NX * GROUP)] * 4,
            out_specs=whole(shape),
        ),
        out_shape=jax.ShapeDtypeStruct(shape, jnp.bfloat16),
        compiler_params=pltpu.CompilerParams(vmem_limit_bytes=VMEM_LIMIT),
    )(slots, acts, *rows)


def output_kernel(slots, weights_ref, act_ref, *out_refs):
    for i in range(STEP):
        expert = pl.program_id(0) * STEP + i
        gate_pre_grad, up_pre_grad, hidden = activations(act_ref, i)
        gate, up, down = [expert_weight(slots, weights_ref, expert, m) for m in range(3)]
        out = lax.dot_general(hidden, down, CONTRACT_ROWS, preferred_element_type=jnp.float32)
        back = lax.dot_general(
            jnp.concatenate([gate_pre_grad, up_pre_grad], axis=0),
            jnp.concatenate([gate, up], axis=0),
            CONTRACT_ROWS,
            preferred_element_type=jnp.float32,
        )
        for b in range(SOURCES):
            part = slice(b * GROUP, (b + 1) * GROUP)
            block = jnp.concatenate([out[part], back[part]], axis=0).astype(jnp.bfloat16)
            if b < NX:
                out_refs[b][i] = block
            else:
                far = (b - NX) * 2 * GROUP
                out_refs[NX][i, far : far + 2 * GROUP] = block


def outputs(slots, weights, acts, experts):
    rows = [2 * GROUP] * NX + [NX * 2 * GROUP]
    return pl.pallas_call(
        output_kernel,
        grid_spec=pltpu.PrefetchScalarGridSpec(
            num_scalar_prefetch=1,
            grid=(experts // STEP,),
            in_specs=[whole(weights.shape), piece_spec()],
            out_specs=[expert_spec(r) for r in rows],
        ),
        out_shape=[jax.ShapeDtypeStruct((experts, r, D_PART), jnp.bfloat16) for r in rows],
        compiler_params=pltpu.CompilerParams(vmem_limit_bytes=VMEM_LIMIT),
    )(slots, weights, acts)


def regroup_matrix(experts, sent):
    e, kind, y, r = np.meshgrid(
        np.arange(experts), np.arange(2), np.arange(NY), np.arange(CAP), indexing="ij"
    )
    source = y * sent + kind * experts * CAP + e * CAP + r
    matrix = np.zeros((source.size, NY * sent), np.float32)
    matrix[np.arange(source.size), source.reshape(-1)] = 1
    return jnp.asarray(matrix, jnp.bfloat16)


def per_device(tokens, expert_ids, gates, tile_slot, w_gate, w_up, w_down, grad_out):
    z_count = lax.axis_size("z")
    tok_rows = tokens.shape[0]
    experts = tile_slot.shape[0] // HTILES
    slot_count = experts * CAP
    sent = -(-2 * slot_count // 16) * 16
    slots = (tile_slot % z_count) * NX + tile_slot // z_count

    weight_parts = swap(weight_slices(w_gate, w_up, w_down), "x")
    weights = lax.all_gather(weight_parts, "z", axis=0, tiled=True)

    route_ids = expert_ids.reshape(-1)
    member = (route_ids[:, None] == jnp.arange(experts, dtype=jnp.int32)[None, :]).astype(jnp.int32)
    slot_rank = jnp.sum((jnp.cumsum(member, axis=0) - member) * member, axis=1)
    position = jnp.where(route_ids < experts, route_ids * CAP + slot_rank, slot_count)
    choose = (position[:, None] == jnp.arange(slot_count, dtype=jnp.int32)[None, :]).astype(
        jnp.float32
    )
    picker = jnp.sum(choose.reshape(tok_rows, TOPK, slot_count), axis=1)
    picker_half = picker.astype(jnp.bfloat16)
    gate_slot = jnp.dot(gates.reshape(-1), choose, precision=lax.Precision.HIGHEST)

    expert_rows = lax.dot_general(
        picker_half, tokens, CONTRACT_ROWS, preferred_element_type=jnp.float32
    ).astype(jnp.bfloat16)
    upstream = lax.dot_general(
        picker_half, grad_out, CONTRACT_ROWS, preferred_element_type=jnp.float32
    )
    scaled = (gate_slot[:, None] * upstream).astype(jnp.bfloat16)
    both = jnp.concatenate([expert_rows, scaled], axis=0)
    both = jnp.pad(both, ((0, sent - 2 * slot_count), (0, 0)))
    both = both.reshape(sent, NY, D_PART).transpose(1, 0, 2)
    regroup = regroup_matrix(experts, sent)
    own_rows = (
        jnp.dot(
            regroup,
            swap(both, "y").reshape(NY * sent, D_PART),
            preferred_element_type=jnp.float32,
        )
        .astype(jnp.bfloat16)
        .reshape(experts, 2 * GROUP, D_PART)
    )
    steps = (1, 3, 2)
    blocks = [own_rows] + [shifted(own_rows, "x", NX, step) for step in steps]
    rows = list(parted_rows(blocks, experts))
    rows = rows + [exchanged(block) for block in rows]

    partial = swap(partial_products(slots, weights, rows, experts), "y")
    pieces = partial.shape[0] // NY
    total = jnp.sum(partial.reshape(NY, pieces, 3 * PACKED, 128).astype(jnp.float32), axis=0)
    pre_gate, pre_up, hidden_grad = [
        total[:, matrix * PACKED : (matrix + 1) * PACKED] for matrix in range(3)
    ]
    sigmoid_gate = jax.nn.sigmoid(pre_gate)
    activated = pre_gate * sigmoid_gate
    acts = jnp.concatenate(
        [
            hidden_grad * pre_up * sigmoid_gate * (1.0 + pre_gate * (1.0 - sigmoid_gate)),
            hidden_grad * activated,
            activated * pre_up,
        ],
        axis=1,
    ).astype(jnp.bfloat16)
    acts = swap(jnp.tile(acts, (NY, 1, 1)), "y")

    grads = weight_grads(slots, acts, rows, experts, z_count * NX)
    grads = lax.psum_scatter(grads, "z", scatter_dimension=0, tiled=True)
    half = D_PART // NC
    grads = grads.reshape(NX, 3 * UNITS, NC, half).transpose(0, 2, 1, 3)
    grads = swap(grads.reshape(NX * NC, 3 * UNITS, half), ("x", "c"))
    grads = grads.reshape(NX * NC, 3, UNITS, half).transpose(1, 0, 2, 3).reshape(3, TILE_W, half)
    gate_weight_grads = grads[0].T[None]
    up_weight_grads = grads[1].T[None]
    down_weight_grads = grads[2][None]

    blocks = outputs(slots, weights, acts, experts)
    far = exchanged(blocks[NX])
    near = [
        (
            block.astype(jnp.float32)
            + far[:, i * 2 * GROUP : (i + 1) * 2 * GROUP].astype(jnp.float32)
        ).astype(jnp.bfloat16)
        for i, block in enumerate(blocks[:NX])
    ]
    home = near[0].astype(jnp.float32)
    for block, step in zip(near[1:], steps, strict=True):
        home = home + shifted(block, "x", NX, NX - step).astype(jnp.float32)
    home = lax.dot_general(
        regroup,
        home.astype(jnp.bfloat16).reshape(experts * 2 * GROUP, D_PART),
        CONTRACT_ROWS,
        preferred_element_type=jnp.float32,
    ).astype(jnp.bfloat16)
    home = swap(home.reshape(NY, sent, D_PART), "y").transpose(1, 0, 2).reshape(sent, D)
    expert_out = home[:slot_count].astype(jnp.float32)
    input_slot = home[slot_count : 2 * slot_count].astype(jnp.float32)
    layer_out = jnp.dot(
        picker, gate_slot[:, None] * expert_out, precision=lax.Precision.HIGHEST
    ).astype(jnp.bfloat16)
    gate_terms = jnp.sum(expert_out * upstream, axis=1)
    gate_grads = jnp.dot(choose, gate_terms, precision=lax.Precision.HIGHEST).reshape(
        tok_rows, TOPK
    )
    token_grads = jnp.dot(picker, input_slot, precision=lax.Precision.HIGHEST).astype(jnp.bfloat16)
    return (
        layer_out,
        token_grads,
        gate_grads,
        gate_weight_grads,
        up_weight_grads,
        down_weight_grads,
    )


def solution(mesh):
    dp, tile = ("y", "c"), ("x", "z")
    planes = Mesh(mesh.devices.reshape(NY, NC, NX, -1), dp + tile)
    rows = P(dp + tile, None)
    in_specs = (
        rows,
        rows,
        rows,
        P(),
        P(tile, None, None),
        P(tile, None, None),
        P(tile, None, None),
        rows,
    )
    out_specs = (
        rows,
        rows,
        rows,
        P(tile, dp, None),
        P(tile, dp, None),
        P(tile, None, dp),
    )
    return jax.shard_map(
        per_device, mesh=planes, in_specs=in_specs, out_specs=out_specs, check_vma=False
    )
```

time: 292 us -> 283 us (0.969)
  the two profiles are of different devices: /device:TPU:321 before, /device:TPU:1 now
where the time goes in v2:
time: 283 us; the launch traced here: 282 us
  waiting for transfers between devices  83.9 us (30%)
  starting transfers between devices  61.8 us (22%)
  blocking collectives  59.3 us (21%)
  Pallas kernels  26.3 us (9%)
  local copies, waits for them, and re-layouts  17.7 us (6%)
  between operations  14.5 us (5%)
  other arithmetic  9.46 us (3%)
  matrix products  8.98 us (3%)
    ppermute x9, waiting for transfers between devices, shifted(): lax.ppermute(value, axis, [(i, (i + step) % size) for i in range(size)])  63.3 us
    all_to_all x4, blocking collectives, swap(): return lax.all_to_all(value, axis, split_axis=0, concat_axis=0, tiled=True)  59.3 us
    ppermute x9, starting transfers between devices, shifted(): lax.ppermute(value, axis, [(i, (i + step) % size) for i in range(size)])  43.8 us
    all_to_all x2, starting transfers between devices, swap(): return lax.all_to_all(value, axis, split_axis=0, concat_axis=0, tiled=True)  17.9 us
    all_to_all x2, waiting for transfers between devices, swap(): return lax.all_to_all(value, axis, split_axis=0, concat_axis=0, tiled=True)  16.9 us
    unnamed x54, local copies, waits for them, and re-layouts  14.4 us
    pallas_call x1, Pallas kernels, partial_products(): pl.pallas_call(partial_kernel, grid_spec=pltpu.PrefetchScalarGridSpec(num...  8.04 us
    pallas_call x1, Pallas kernels, outputs(): pl.pallas_call(output_kernel, grid_spec=pltpu.PrefetchScalarGridSpec(num_...  7.86 us
  transfers between devices with their start and end apart: 13, of which 10 were waited for; matrix products, arithmetic and copies ran while one was open for 7% of the time, Pallas kernels for 3%

profile of v2, /device:TPU:1, one launch (start us, length us, event | category | flops | bytes accessed | tf_op | source)
XLA Modules:
  0.0 281.8 jit_solution(13711672242204974877)
XLA Ops:
  11.0 9.9 %all_to_all.30 = bf16[4,48,512]{2,1,0:T(8,128)(2,1)} all-to-all(bf16[4,48,512]{2,1,0:T(8,128)(2,1)S(1)} %shard_map.136), channel_id=1, replica_groups=mesh['y'=4,'c'=2,'x'=4,'z'=16] {'x'}, dimensions={0} | all-to-all | bytes 393216 | tf_op jit(solution)/shard_map/all_to_all | solution.py:39
  21.3 2.8 %reduce-window.6 = s32[10,8,128]{2,1,0:T(8,128)S(1)} reduce-window(s32[10,8,128]{2,1,0:T(8,128)S(1)} %fusion.10, s32[]{:T(128)} %constant.36.clone.1), window={size=1x1x128 pad=0_0x0_0x127_0}, to_apply=%region_0.1 | reduce-window | flops 1300480 | bytes 81924 | tf_op jit(solution)/shard_map/reduce-window
  27.3 12.8 %all_to_all.31 = bf16[4,208,512]{2,1,0:T(8,128)(2,1)S(1)} all-to-all(bf16[4,208,512]{2,1,0:T(8,128)(2,1)S(1)} %bitcast.79), channel_id=1, replica_groups=mesh['y'=4,'c'=2,'x'=4,'z'=16] {'y'}, dimensions={0} | all-to-all | bytes 1703936 | tf_op jit(solution)/shard_map/all_to_all | solution.py:39
  43.4 4.2 %collective-permute-start.1 = (bf16[10,80,512]{2,1,0:T(8,128)(2,1)S(1)}, bf16[10,80,512]{2,1,0:T(8,128)(2,1)S(1)}, u32[]{:S(2)}, u32[]{:S(2)}) collective-permute-start(bf16[10,80,512]{2,1,0:T(8,128)(2,1)S(1)} %bitcast.69), channel_id=1, source_target_pairs={{0,48},{16,0},{32,16},{48,32},{1,49},{17,1},{33,17},{49,33},{2,50}... | collective-permute-start | bytes 2457608 | tf_op jit(solution)/shard_map/ppermute | solution.py:31
  49.5 9.1 %collective-permute-done.refs_1_ = bf16[10,80,512]{2,1,0:T(8,128)(2,1)S(1)} collective-permute-done((bf16[10,80,512]{2,1,0:T(8,128)(2,1)S(1)}, bf16[10,80,512]{2,1,0:T(8,128)(2,1)S(1)}, u32[]{:S(2)}, u32[]{:S(2)}) %collective-permute-start) | collective-permute-done | bytes 819232 | tf_op jit(solution)/shard_map/ppermute | solution.py:31
  59.5 15.6 %collective-permute-done.2.refs_3_ = bf16[10,80,512]{2,1,0:T(8,128)(2,1)S(1)} collective-permute-done((bf16[10,80,512]{2,1,0:T(8,128)(2,1)S(1)}, bf16[10,80,512]{2,1,0:T(8,128)(2,1)S(1)}, u32[]{:S(2)}, u32[]{:S(2)}) %collective-permute-start.2) | collective-permute-done | bytes 819232 | tf_op jit(solution)/shard_map/ppermute | solution.py:31
  75.1 2.3 shard_map.137
  77.4 10.5 %collective-permute-start.3 = (bf16[10,160,512]{2,1,0:T(8,128)(2,1)S(1)}, bf16[10,160,512]{2,1,0:T(8,128)(2,1)S(1)}, u32[]{:S(2)}, u32[]{:S(2)}) collective-permute-start(bf16[10,160,512]{2,1,0:T(8,128)(2,1)S(1)} %get-tuple-element.13.refs_0_), channel_id=1, source_target_pairs={{0,64},{64,0},{1,65},{65,1},{2,66},{66,2},{3,67},{67,3},{4,68},{68... | collective-permute-start | bytes 4915208 | tf_op jit(solution)/shard_map/ppermute | solution.py:31
  96.5 8.0 %shard_map.138 = bf16[20,360,128]{2,1,0:T(8,128)(2,1)} custom-call(s32[60]{0:T(128)S(1)} %fusion.15.slots, bf16[64,48,512]{2,1,0:T(8,128)(2,1)} %all-gather.2.cloned.1.call-done.weights_ref, bf16[10,160,512]{2,1,0:T(8,128)(2,1)S(1)} %get-tuple-element.13.refs_0_, bf16[10,160,512]{2,1,0:T(8,128)(2,1)S(1)} %copy-done.2, bf16[10,160,512]{2,1,0:T(8,128)(2,1)S(1)} %copy-done.5, ...), custom_call_target="tpu_custom_call" | custom-call | tf_op jit(solution)/shard_map/pallas_call | solution.py:150
  104.6 17.9 %all_to_all.32 = bf16[20,360,128]{2,1,0:T(8,128)(2,1)S(1)} all-to-all(bf16[20,360,128]{2,1,0:T(8,128)(2,1)} %shard_map.138), channel_id=1, replica_groups=mesh['y'=4,'c'=2,'x'=4,'z'=16] {'y'}, dimensions={0} | all-to-all | bytes 3686400 | tf_op jit(solution)/shard_map/all_to_all | solution.py:39
  123.2 18.7 %all_to_all.33.act_ref = bf16[20,360,128]{2,1,0:T(8,128)(2,1)S(1)} all-to-all(bf16[20,360,128]{2,1,0:T(8,128)(2,1)S(1)} %bitcast.75), channel_id=1, replica_groups=mesh['y'=4,'c'=2,'x'=4,'z'=16] {'y'}, dimensions={0} | all-to-all | bytes 3686400 | tf_op jit(solution)/shard_map/all_to_all | solution.py:39
  141.9 7.9 %shard_map.139 = (bf16[10,80,512]{2,1,0:T(8,128)(2,1)S(1)}, bf16[10,80,512]{2,1,0:T(8,128)(2,1)S(1)}, bf16[10,80,512]{2,1,0:T(8,128)(2,1)S(1)}, bf16[10,80,512]{2,1,0:T(8,128)(2,1)S(1)}, bf16[10,320,512]{2,1,0:T(8,128)(2,1)}) custom-call(s32[60]{0:T(128)S(1)} %fusion.15.slots, bf16[64,48,512]{2,1,0:T(8,128)(2,1)} %all-gather.2.cloned.1.call-done.weights_ref, ...), custom_call_target="tpu_custom_call" | custom-call | tf_op jit(solution)/shard_map/pallas_call | solution.py:234
  152.5 13.2 %collective-permute-start.5 = (bf16[10,320,512]{2,1,0:T(8,128)(2,1)}, bf16[10,320,512]{2,1,0:T(8,128)(2,1)}, u32[]{:S(2)}, u32[]{:S(2)}) collective-permute-start(bf16[10,320,512]{2,1,0:T(8,128)(2,1)} %get-tuple-element.16), channel_id=1, source_target_pairs={{0,64},{64,0},{1,65},{65,1},{2,66},{66,2},{3,67},{67,3},{4,68},{68... | collective-permute-start | bytes 9830408 | tf_op jit(solution)/shard_map/ppermute | solution.py:31
  165.7 7.4 %shard_map.140 = bf16[64,48,512]{2,1,0:T(8,128)(2,1)} custom-call(s32[60]{0:T(128)S(1)} %fusion.15.slots, bf16[20,360,128]{2,1,0:T(8,128)(2,1)} %copy-done.1, bf16[10,160,512]{2,1,0:T(8,128)(2,1)S(1)} %get-tuple-element.13.refs_0_, bf16[10,160,512]{2,1,0:T(8,128)(2,1)S(1)} %copy-done.3, bf16[10,160,512]{2,1,0:T(8,128)(2,1)S(1)} %copy-done.6, ...), custom_call_target="tpu_custom_call" | custom-call | tf_op jit(solution)/shard_map/pallas_call | solution.py:197
  174.6 2.8 add_convert_fusion.3
  177.3 4.5 %collective-permute-start.6 = (bf16[10,80,512]{2,1,0:T(8,128)(2,1)S(1)}, bf16[10,80,512]{2,1,0:T(8,128)(2,1)S(1)}, u32[]{:S(2)}, u32[]{:S(2)}) collective-permute-start(bf16[10,80,512]{2,1,0:T(8,128)(2,1)S(1)} %get-tuple-element.56), channel_id=1, source_target_pairs={{0,48},{16,0},{32,16},{48,32},{1,49},{17,1},{33,17},{49,33},{2,50}... | collective-permute-start | bytes 2457608 | tf_op jit(solution)/shard_map/ppermute | solution.py:31
  183.8 3.4 %collective-permute-start.8 = (bf16[10,80,512]{2,1,0:T(8,128)(2,1)S(1)}, bf16[10,80,512]{2,1,0:T(8,128)(2,1)S(1)}, u32[]{:S(2)}, u32[]{:S(2)}) collective-permute-start(bf16[10,80,512]{2,1,0:T(8,128)(2,1)S(1)} %get-tuple-element.57), channel_id=1, source_target_pairs={{0,32},{16,48},{32,0},{48,16},{1,33},{17,49},{33,1},{49,17},{2,34}... | collective-permute-start | bytes 2457608 | tf_op jit(solution)/shard_map/ppermute | solution.py:31
  187.2 29.8 %collective-permute-done.6 = bf16[10,80,512]{2,1,0:T(8,128)(2,1)S(1)} collective-permute-done((bf16[10,80,512]{2,1,0:T(8,128)(2,1)S(1)}, bf16[10,80,512]{2,1,0:T(8,128)(2,1)S(1)}, u32[]{:S(2)}, u32[]{:S(2)}) %collective-permute-start.6) | collective-permute-done | bytes 819232 | tf_op jit(solution)/shard_map/ppermute | solution.py:31
  217.0 5.3 %collective-permute-done.7 = bf16[10,80,512]{2,1,0:T(8,128)(2,1)S(1)} collective-permute-done((bf16[10,80,512]{2,1,0:T(8,128)(2,1)S(1)}, bf16[10,80,512]{2,1,0:T(8,128)(2,1)S(1)}, u32[]{:S(2)}, u32[]{:S(2)}) %collective-permute-start.7) | collective-permute-done | bytes 819232 | tf_op jit(solution)/shard_map/ppermute | solution.py:31
  226.1 3.7 %all-to-all-start.4 = ((bf16[4,208,512]{2,1,0:T(8,128)(2,1)}), bf16[4,208,512]{2,1,0:T(8,128)(2,1)S(1)}, u32[]{:S(2)}, u32[]{:S(2)}) async-start(bf16[4,208,512]{2,1,0:T(8,128)(2,1)} %bitcast.12), calls=%async_computation.4 | async-start | bytes 1703936 | tf_op jit(solution)/shard_map/all_to_all | solution.py:39
  229.9 11.8 %all-to-all-done.4 = bf16[4,208,512]{2,1,0:T(8,128)(2,1)S(1)} async-done(((bf16[4,208,512]{2,1,0:T(8,128)(2,1)}), bf16[4,208,512]{2,1,0:T(8,128)(2,1)S(1)}, u32[]{:S(2)}, u32[]{:S(2)}) %all-to-all-start.4) | async-done | bytes 852000 | tf_op jit(solution)/shard_map/all_to_all | solution.py:39
  247.4 3.7 %reduce-scatter.2.cloned.1.call-done = bf16[4,48,512]{2,1,0:T(8,128)(2,1)} async-done(((bf16[64,48,512]{2,1,0:T(8,128)(2,1)}), bf16[4,48,512]{2,1,0:T(8,128)(2,1)}) %reduce-scatter.2.cloned.1.call-update) | async-done | bytes 196624 | tf_op jit(solution)/shard_map/reduce_scatter | solution.py:323
  252.8 14.2 %all-to-all-start.5 = ((bf16[8,48,256]{2,1,0:T(8,128)(2,1)}), bf16[8,48,256]{2,1,0:T(8,128)(2,1)S(1)}, u32[]{:S(2)}, u32[]{:S(2)}) async-start(bf16[8,48,256]{2,1,0:T(8,128)(2,1)} %bitcast.16), calls=%async_computation.6 | async-start | bytes 393216 | tf_op jit(solution)/shard_map/all_to_all | solution.py:39
  267.8 5.1 %all-to-all-done.5 = bf16[8,48,256]{2,1,0:T(8,128)(2,1)S(1)} async-done(((bf16[8,48,256]{2,1,0:T(8,128)(2,1)}), bf16[8,48,256]{2,1,0:T(8,128)(2,1)S(1)}, u32[]{:S(2)}, u32[]{:S(2)}) %all-to-all-start.5) | async-done | bytes 196640 | tf_op jit(solution)/shard_map/all_to_all | solution.py:39
  (109 shorter events, 42.8 us)
Async XLA Ops:
  7.2 18.7 %copy-start = (bf16[128,2048]{1,0:T(8,128)(2,1)S(1)}, bf16[128,2048]{1,0:T(8,128)(2,1)}, u32[]{:S(2)}) copy-start(bf16[128,2048]{1,0:T(8,128)(2,1)} %param.16) | copy-start | bytes 1572868
  7.2 86.5 %all-gather.2.cloned.1.call-start = ((), (), s32[]{:S(2)}) async-start(), calls=%async_computation.7 | async-start | bytes 3342336 | tf_op jit(solution)/shard_map/all_gather | solution.py:266
  10.4 10.6 %copy-start.17 = (s32[128,8]{0,1:T(8,128)S(1)}, s32[128,8]{0,1:T(8,128)}, u32[]{:S(2)}) copy-start(s32[128,8]{0,1:T(8,128)} %param.10) | copy-start | bytes 12292
  10.4 14.4 %copy-start.18 = (f32[128,8]{0,1:T(8,128)S(1)}, f32[128,8]{0,1:T(8,128)}, u32[]{:S(2)}) copy-start(f32[128,8]{0,1:T(8,128)} %param.11) | copy-start | bytes 12292
  10.4 15.1 %copy-start.16 = (bf16[128,2048]{1,0:T(8,128)(2,1)S(1)}, bf16[128,2048]{1,0:T(8,128)(2,1)}, u32[]{:S(2)}) copy-start(bf16[128,2048]{1,0:T(8,128)(2,1)} %param.9) | copy-start | bytes 1572868
  21.0 230.2 %reduce-scatter.2.cloned.1.call-start = ((), (), s32[]{:S(2)}) async-start(), calls=%async_computation.8 | async-start | bytes 3342336 | tf_op jit(solution)/shard_map/reduce_scatter | solution.py:323
  27.2 12.9 %copy-start.20 = (bf16[800,832]{1,0:T(8,128)(2,1)S(1)}, bf16[800,832]{1,0:T(8,128)(2,1)}, u32[]{:S(2)}) copy-start(bf16[800,832]{1,0:T(8,128)(2,1)} %constant.46.clone) | copy-start | bytes 3993604
  41.1 48.7 %copy-start.19 = (s32[60]{0:T(128)S(1)}, s32[60]{0:T(128)}, u32[]{:S(2)}) copy-start(s32[60]{0:T(128)} %param.12) | copy-start | bytes 724
  41.1 17.6 %collective-permute-start = (bf16[10,80,512]{2,1,0:T(8,128)(2,1)S(1)}, bf16[10,80,512]{2,1,0:T(8,128)(2,1)S(1)}, u32[]{:S(2)}, u32[]{:S(2)}) collective-permute-start(bf16[10,80,512]{2,1,0:T(8,128)(2,1)S(1)} %bitcast.68), channel_id=1, source_target_pairs={{0,16},{16,32},{32,48},{48,0},{1,17},{17,33},{33,49},{49,1},{2,18}... | collective-permute-start | bytes 2457608 | tf_op jit(solution)/shard_map/ppermute | solution.py:31
  43.4 16.1 %collective-permute-start.1 = (bf16[10,80,512]{2,1,0:T(8,128)(2,1)S(1)}, bf16[10,80,512]{2,1,0:T(8,128)(2,1)S(1)}, u32[]{:S(2)}, u32[]{:S(2)}) collective-permute-start(bf16[10,80,512]{2,1,0:T(8,128)(2,1)S(1)} %bitcast.69), channel_id=1, source_target_pairs={{0,48},{16,0},{32,16},{48,32},{1,49},{17,1},{33,17},{49,33},{2,50}... | collective-permute-start | bytes 2457608 | tf_op jit(solution)/shard_map/ppermute | solution.py:31
  47.6 27.5 %collective-permute-start.2 = (bf16[10,80,512]{2,1,0:T(8,128)(2,1)S(1)}, bf16[10,80,512]{2,1,0:T(8,128)(2,1)S(1)}, u32[]{:S(2)}, u32[]{:S(2)}) collective-permute-start(bf16[10,80,512]{2,1,0:T(8,128)(2,1)S(1)} %bitcast.70), channel_id=1, source_target_pairs={{0,32},{16,48},{32,0},{48,16},{1,33},{17,49},{33,1},{49,17},{2,34}... | collective-permute-start | bytes 2457608 | tf_op jit(solution)/shard_map/ppermute | solution.py:31
  77.4 13.6 %collective-permute-start.3 = (bf16[10,160,512]{2,1,0:T(8,128)(2,1)S(1)}, bf16[10,160,512]{2,1,0:T(8,128)(2,1)S(1)}, u32[]{:S(2)}, u32[]{:S(2)}) collective-permute-start(bf16[10,160,512]{2,1,0:T(8,128)(2,1)S(1)} %get-tuple-element.13.refs_0_), channel_id=1, source_target_pairs={{0,64},{64,0},{1,65},{65,1},{2,66},{66,2},{3,67},{67,3},{4,68},{68... | collective-permute-start | bytes 4915208 | tf_op jit(solution)/shard_map/ppermute | solution.py:31
  87.9 5.8 %collective-permute-start.4 = (bf16[10,160,512]{2,1,0:T(8,128)(2,1)}, bf16[10,160,512]{2,1,0:T(8,128)(2,1)}, u32[]{:S(2)}, u32[]{:S(2)}) collective-permute-start(bf16[10,160,512]{2,1,0:T(8,128)(2,1)} %get-tuple-element.14.refs_1_), channel_id=1, source_target_pairs={{0,64},{64,0},{1,65},{65,1},{2,66},{66,2},{3,67},{67,3},{4,68},{68... | collective-permute-start | bytes 4915208 | tf_op jit(solution)/shard_map/ppermute | solution.py:31
  93.7 1.4 copy-start.2
  141.9 7.9 %copy-start.1 = (bf16[20,360,128]{2,1,0:T(8,128)(2,1)}, bf16[20,360,128]{2,1,0:T(8,128)(2,1)S(1)}, u32[]{:S(2)}) copy-start(bf16[20,360,128]{2,1,0:T(8,128)(2,1)S(1)} %all_to_all.33.act_ref) | copy-start | bytes 5529604
  141.9 23.8 %copy-start.3 = (bf16[10,160,512]{2,1,0:T(8,128)(2,1)S(1)}, bf16[10,160,512]{2,1,0:T(8,128)(2,1)}, u32[]{:S(2)}) copy-start(bf16[10,160,512]{2,1,0:T(8,128)(2,1)} %get-tuple-element.14.refs_1_) | copy-start | bytes 4915204
  141.9 23.9 %copy-start.6 = (bf16[10,160,512]{2,1,0:T(8,128)(2,1)S(1)}, bf16[10,160,512]{2,1,0:T(8,128)(2,1)}, u32[]{:S(2)}) copy-start(bf16[10,160,512]{2,1,0:T(8,128)(2,1)} %copy-done.4) | copy-start | bytes 4915204
  152.5 20.7 %collective-permute-start.5 = (bf16[10,320,512]{2,1,0:T(8,128)(2,1)}, bf16[10,320,512]{2,1,0:T(8,128)(2,1)}, u32[]{:S(2)}, u32[]{:S(2)}) collective-permute-start(bf16[10,320,512]{2,1,0:T(8,128)(2,1)} %get-tuple-element.16), channel_id=1, source_target_pairs={{0,64},{64,0},{1,65},{65,1},{2,66},{66,2},{3,67},{67,3},{4,68},{68... | collective-permute-start | bytes 9830408 | tf_op jit(solution)/shard_map/ppermute | solution.py:31
  177.3 39.6 %collective-permute-start.6 = (bf16[10,80,512]{2,1,0:T(8,128)(2,1)S(1)}, bf16[10,80,512]{2,1,0:T(8,128)(2,1)S(1)}, u32[]{:S(2)}, u32[]{:S(2)}) collective-permute-start(bf16[10,80,512]{2,1,0:T(8,128)(2,1)S(1)} %get-tuple-element.56), channel_id=1, source_target_pairs={{0,48},{16,0},{32,16},{48,32},{1,49},{17,1},{33,17},{49,33},{2,50}... | collective-permute-start | bytes 2457608 | tf_op jit(solution)/shard_map/ppermute | solution.py:31
  181.8 40.4 %collective-permute-start.7 = (bf16[10,80,512]{2,1,0:T(8,128)(2,1)S(1)}, bf16[10,80,512]{2,1,0:T(8,128)(2,1)S(1)}, u32[]{:S(2)}, u32[]{:S(2)}) collective-permute-start(bf16[10,80,512]{2,1,0:T(8,128)(2,1)S(1)} %get-tuple-element.58), channel_id=1, source_target_pairs={{0,16},{16,32},{32,48},{48,0},{1,17},{17,33},{33,49},{49,1},{2,18}... | collective-permute-start | bytes 2457608 | tf_op jit(solution)/shard_map/ppermute | solution.py:31
  183.8 38.4 %collective-permute-start.8 = (bf16[10,80,512]{2,1,0:T(8,128)(2,1)S(1)}, bf16[10,80,512]{2,1,0:T(8,128)(2,1)S(1)}, u32[]{:S(2)}, u32[]{:S(2)}) collective-permute-start(bf16[10,80,512]{2,1,0:T(8,128)(2,1)S(1)} %get-tuple-element.57), channel_id=1, source_target_pairs={{0,32},{16,48},{32,0},{48,16},{1,33},{17,49},{33,1},{49,17},{2,34}... | collective-permute-start | bytes 2457608 | tf_op jit(solution)/shard_map/ppermute | solution.py:31
  222.2 1.9 copy-start.21
  226.1 15.6 %all-to-all-start.4 = ((bf16[4,208,512]{2,1,0:T(8,128)(2,1)}), bf16[4,208,512]{2,1,0:T(8,128)(2,1)S(1)}, u32[]{:S(2)}, u32[]{:S(2)}) async-start(bf16[4,208,512]{2,1,0:T(8,128)(2,1)} %bitcast.12), calls=%async_computation.4 | async-start | bytes 1703936 | tf_op jit(solution)/shard_map/all_to_all | solution.py:39
  252.8 20.1 %all-to-all-start.5 = ((bf16[8,48,256]{2,1,0:T(8,128)(2,1)}), bf16[8,48,256]{2,1,0:T(8,128)(2,1)S(1)}, u32[]{:S(2)}, u32[]{:S(2)}) async-start(bf16[8,48,256]{2,1,0:T(8,128)(2,1)} %bitcast.16), calls=%async_computation.6 | async-start | bytes 393216 | tf_op jit(solution)/shard_map/all_to_all | solution.py:39
  (11 other events, 12.2 us)
Sparse Core Ops, SparseCore 0:
  21.1 71.5 all-gather.1
  173.3 77.7 reduce-scatter.1

commit v3 on v2

--- a/solution.py
+++ b/solution.py
@@ -1,3 +1,5 @@
+import functools
+
 import jax
 import jax.numpy as jnp
 import numpy as np
@@ -21,7 +23,10 @@
 LANES = SOURCES * GROUP
 PACKED = HALF * LANES // 128
 STEP = 2
-VMEM_LIMIT = 48 * 1024 * 1024
+VMEM_LIMIT = 20 * 1024 * 1024
+WIDE_VMEM_LIMIT = 60 * 1024 * 1024
+PARTS = ((0, 6), (6, 4))
+STEPS = (1, 3, 2)
 
 CONTRACT_COLS = (((1,), (1,)), ((), ()))
 CONTRACT_ROWS = (((0,), (0,)), ((), ()))
@@ -66,7 +71,7 @@
 def weight_slices(w_gate, w_up, w_down):
     return pl.pallas_call(
         slice_kernel,
-        in_specs=[pl.BlockSpec(memory_space=pltpu.HBM)] * 3,
+        in_specs=[pl.BlockSpec(memory_space=pl.ANY)] * 3,
         out_shape=jax.ShapeDtypeStruct((NX, 3 * UNITS, D_PART), jnp.bfloat16),
         scratch_shapes=[
             pltpu.VMEM((D_PART, TILE_W), jnp.bfloat16),
@@ -75,7 +80,7 @@
             pltpu.VMEM((TILE_W, D_PART), jnp.bfloat16),
             pltpu.SemaphoreType.DMA((3,)),
         ],
-        compiler_params=pltpu.CompilerParams(vmem_limit_bytes=VMEM_LIMIT),
+        compiler_params=pltpu.CompilerParams(vmem_limit_bytes=WIDE_VMEM_LIMIT),
     )(w_gate, w_up, w_down)
 
 
@@ -101,8 +106,8 @@
     return pl.BlockSpec((STEP, rows, D_PART), lambda e, *_: (e, 0, 0))
 
 
-def piece_spec():
-    return pl.BlockSpec((2 * STEP, 3 * PACKED, 128), lambda e, *_: (e, 0, 0))
+def piece_spec(first=0):
+    return pl.BlockSpec((2 * STEP, 3 * PACKED, 128), lambda e, *_: (e + first // STEP, 0, 0))
 
 
 def expert_weight(slots, weights_ref, expert, matrix):
@@ -124,37 +129,39 @@
     return jnp.concatenate([values[:HALF], values[HALF : 2 * HALF], rest], axis=1)
 
 
-def partial_kernel(slots, weights_ref, *refs):
-    near_inputs, near_scaled, far_inputs, far_scaled, out_ref = refs
-    for i in range(STEP):
-        expert = pl.program_id(0) * STEP + i
-        inputs = jnp.concatenate([near_inputs[i], far_inputs[i]], axis=0)
-        scaled = jnp.concatenate([near_scaled[i], far_scaled[i]], axis=0)
-        products = [
-            lax.dot_general(
-                expert_weight(slots, weights_ref, expert, matrix),
-                rows,
-                CONTRACT_COLS,
-                preferred_element_type=jnp.float32,
-            )
-            for matrix, rows in ((0, inputs), (1, inputs), (2, scaled))
-        ]
+def partial_kernel(experts, slots, weights, near_inputs, near_scaled, far_inputs, far_scaled, out):
+    for expert in range(experts):
+        gate, up, down = [expert_weight(slots, weights, expert, m) for m in range(3)]
+        both = lax.dot_general(
+            jnp.concatenate([gate, up], axis=0),
+            jnp.concatenate([near_inputs[expert], far_inputs[expert]], axis=0),
+            CONTRACT_COLS,
+            preferred_element_type=jnp.float32,
+        )
+        grad = lax.dot_general(
+            down,
+            jnp.concatenate([near_scaled[expert], far_scaled[expert]], axis=0),
+            CONTRACT_COLS,
+            preferred_element_type=jnp.float32,
+        )
+        products = both[: 2 * HALF], both[2 * HALF :], grad
         for half in range(2):
             part = slice(half * HALF, (half + 1) * HALF)
-            out_ref[2 * i + half] = jnp.concatenate(
+            out[2 * expert + half] = jnp.concatenate(
                 [packed(p[part]) for p in products], axis=0
             ).astype(jnp.bfloat16)
 
 
+def in_vmem(count):
+    smem = pl.BlockSpec(memory_space=pltpu.SMEM)
+    return [smem] + [pl.BlockSpec(memory_space=pltpu.VMEM)] * count
+
+
 def partial_products(slots, weights, rows, experts):
     return pl.pallas_call(
-        partial_kernel,
-        grid_spec=pltpu.PrefetchScalarGridSpec(
-            num_scalar_prefetch=1,
-            grid=(experts // STEP,),
-            in_specs=[whole(weights.shape)] + [expert_spec(NX * GROUP)] * 4,
-            out_specs=piece_spec(),
-        ),
+        functools.partial(partial_kernel, experts),
+        in_specs=in_vmem(5),
+        out_specs=pl.BlockSpec(memory_space=pltpu.VMEM),
         out_shape=jax.ShapeDtypeStruct((2 * experts, 3 * PACKED, 128), jnp.bfloat16),
         compiler_params=pltpu.CompilerParams(vmem_limit_bytes=VMEM_LIMIT),
     )(slots, weights, *rows)
@@ -170,46 +177,47 @@
     ]
 
 
-def weight_grad_kernel(slots, act_ref, *refs):
-    near_inputs, near_scaled, far_inputs, far_scaled, out_ref = refs
-
-    @pl.when(pl.program_id(0) == 0)
-    def _():
-        out_ref[...] = jnp.zeros_like(out_ref)
-
-    for i in range(STEP):
-        expert = pl.program_id(0) * STEP + i
-        inputs = jnp.concatenate([near_inputs[i], far_inputs[i]], axis=0)
-        scaled = jnp.concatenate([near_scaled[i], far_scaled[i]], axis=0)
-        acts = activations(act_ref, i)
-        for matrix, rows in enumerate((inputs, inputs, scaled)):
-            grad = jnp.dot(acts[matrix], rows, preferred_element_type=jnp.float32)
-            grad = grad.astype(jnp.bfloat16)
+def weight_grad_kernel(
+    experts, slots, acts, near_inputs, near_scaled, far_inputs, far_scaled, out
+):
+    out[...] = jnp.zeros_like(out)
+    half = D_PART // NC
+    for expert in range(experts):
+        gate_pre_grad, up_pre_grad, hidden = activations(acts, expert)
+        both = jnp.dot(
+            jnp.concatenate([gate_pre_grad, up_pre_grad], axis=0),
+            jnp.concatenate([near_inputs[expert], far_inputs[expert]], axis=0),
+            preferred_element_type=jnp.float32,
+        ).astype(jnp.bfloat16)
+        down = jnp.dot(
+            hidden,
+            jnp.concatenate([near_scaled[expert], far_scaled[expert]], axis=0),
+            preferred_element_type=jnp.float32,
+        ).astype(jnp.bfloat16)
+        for matrix, part in enumerate((both[: 2 * HALF], both[2 * HALF :], down)):
+            rows = slice(matrix * UNITS, (matrix + 1) * UNITS)
             for h in range(HTILES):
+                units = part[h * UNITS : (h + 1) * UNITS]
                 slot = slots[expert * HTILES + h]
-                out_ref[slot, matrix * UNITS : (matrix + 1) * UNITS, :] = grad[
-                    h * UNITS : (h + 1) * UNITS
-                ]
+                for c in range(NC):
+                    out[slot * NC + c, rows, :] = units[:, c * half : (c + 1) * half]
 
 
 def weight_grads(slots, acts, rows, experts, tile_count):
-    shape = (tile_count, 3 * UNITS, D_PART)
-    return pl.pallas_call(
-        weight_grad_kernel,
-        grid_spec=pltpu.PrefetchScalarGridSpec(
-            num_scalar_prefetch=1,
-            grid=(experts // STEP,),
-            in_specs=[piece_spec()] + [expert_spec(NX * GROUP)] * 4,
-            out_specs=whole(shape),
+    return pl.pallas_call(
+        functools.partial(weight_grad_kernel, experts),
+        in_specs=in_vmem(5),
+        out_specs=pl.BlockSpec(memory_space=pltpu.VMEM),
+        out_shape=jax.ShapeDtypeStruct(
+            (tile_count * NC, 3 * UNITS, D_PART // NC), jnp.bfloat16
         ),
-        out_shape=jax.ShapeDtypeStruct(shape, jnp.bfloat16),
         compiler_params=pltpu.CompilerParams(vmem_limit_bytes=VMEM_LIMIT),
     )(slots, acts, *rows)
 
 
-def output_kernel(slots, weights_ref, act_ref, *out_refs):
+def output_kernel(first, slots, weights_ref, act_ref, *out_refs):
     for i in range(STEP):
-        expert = pl.program_id(0) * STEP + i
+        expert = first + pl.program_id(0) * STEP + i
         gate_pre_grad, up_pre_grad, hidden = activations(act_ref, i)
         gate, up, down = [expert_weight(slots, weights_ref, expert, m) for m in range(3)]
         out = lax.dot_general(hidden, down, CONTRACT_ROWS, preferred_element_type=jnp.float32)
@@ -229,14 +237,14 @@
                 out_refs[NX][i, far : far + 2 * GROUP] = block
 
 
-def outputs(slots, weights, acts, experts):
+def outputs(slots, weights, acts, first, experts):
     rows = [2 * GROUP] * NX + [NX * 2 * GROUP]
     return pl.pallas_call(
-        output_kernel,
+        functools.partial(output_kernel, first),
         grid_spec=pltpu.PrefetchScalarGridSpec(
             num_scalar_prefetch=1,
             grid=(experts // STEP,),
-            in_specs=[whole(weights.shape), piece_spec()],
+            in_specs=[whole(weights.shape), piece_spec(first)],
             out_specs=[expert_spec(r) for r in rows],
         ),
         out_shape=[jax.ShapeDtypeStruct((experts, r, D_PART), jnp.bfloat16) for r in rows],
@@ -254,12 +262,55 @@
     return jnp.asarray(matrix, jnp.bfloat16)
 
 
+def tile_grad_kernel(parts, gate, up, down):
+    for matrix, ref in enumerate((gate, up, down)):
+        rows = slice(matrix * UNITS, (matrix + 1) * UNITS)
+        whole_tile = jnp.concatenate([parts[i, rows, :] for i in range(SOURCES)], axis=0)
+        ref[0] = whole_tile if matrix == 2 else whole_tile.T
+
+
+def tile_grads(parts):
+    half = parts.shape[2]
+    turned = jax.ShapeDtypeStruct((1, half, TILE_W), jnp.bfloat16)
+    return pl.pallas_call(
+        tile_grad_kernel,
+        out_shape=[turned, turned, jax.ShapeDtypeStruct((1, TILE_W, half), jnp.bfloat16)],
+        compiler_params=pltpu.CompilerParams(vmem_limit_bytes=VMEM_LIMIT),
+    )(parts)
+
+
+def sent_rows(experts):
+    return -(-2 * experts * CAP // 16) * 16
+
+
+def send_home(blocks, experts):
+    sent = sent_rows(experts)
+    far = exchanged(blocks[NX])
+    near = [
+        (
+            block.astype(jnp.float32)
+            + far[:, i * 2 * GROUP : (i + 1) * 2 * GROUP].astype(jnp.float32)
+        ).astype(jnp.bfloat16)
+        for i, block in enumerate(blocks[:NX])
+    ]
+    home = near[0].astype(jnp.float32)
+    for block, step in zip(near[1:], STEPS, strict=True):
+        home = home + shifted(block, "x", NX, NX - step).astype(jnp.float32)
+    home = lax.dot_general(
+        regroup_matrix(experts, sent),
+        home.astype(jnp.bfloat16).reshape(experts * 2 * GROUP, D_PART),
+        CONTRACT_ROWS,
+        preferred_element_type=jnp.float32,
+    ).astype(jnp.bfloat16)
+    return swap(home.reshape(NY, sent, D_PART), "y").transpose(1, 0, 2).reshape(sent, D)
+
+
 def per_device(tokens, expert_ids, gates, tile_slot, w_gate, w_up, w_down, grad_out):
     z_count = lax.axis_size("z")
     tok_rows = tokens.shape[0]
     experts = tile_slot.shape[0] // HTILES
     slot_count = experts * CAP
-    sent = -(-2 * slot_count // 16) * 16
+    sent = sent_rows(experts)
     slots = (tile_slot % z_count) * NX + tile_slot // z_count
 
     weight_parts = swap(weight_slices(w_gate, w_up, w_down), "x")
@@ -296,8 +347,7 @@
         .astype(jnp.bfloat16)
         .reshape(experts, 2 * GROUP, D_PART)
     )
-    steps = (1, 3, 2)
-    blocks = [own_rows] + [shifted(own_rows, "x", NX, step) for step in steps]
+    blocks = [own_rows] + [shifted(own_rows, "x", NX, step) for step in STEPS]
     rows = list(parted_rows(blocks, experts))
     rows = rows + [exchanged(block) for block in rows]
 
@@ -320,44 +370,25 @@
     acts = swap(jnp.tile(acts, (NY, 1, 1)), "y")
 
     grads = weight_grads(slots, acts, rows, experts, z_count * NX)
-    grads = lax.psum_scatter(grads, "z", scatter_dimension=0, tiled=True)
-    half = D_PART // NC
-    grads = grads.reshape(NX, 3 * UNITS, NC, half).transpose(0, 2, 1, 3)
-    grads = swap(grads.reshape(NX * NC, 3 * UNITS, half), ("x", "c"))
-    grads = grads.reshape(NX * NC, 3, UNITS, half).transpose(1, 0, 2, 3).reshape(3, TILE_W, half)
-    gate_weight_grads = grads[0].T[None]
-    up_weight_grads = grads[1].T[None]
-    down_weight_grads = grads[2][None]
-
-    blocks = outputs(slots, weights, acts, experts)
-    far = exchanged(blocks[NX])
-    near = [
-        (
-            block.astype(jnp.float32)
-            + far[:, i * 2 * GROUP : (i + 1) * 2 * GROUP].astype(jnp.float32)
-        ).astype(jnp.bfloat16)
-        for i, block in enumerate(blocks[:NX])
-    ]
-    home = near[0].astype(jnp.float32)
-    for block, step in zip(near[1:], steps, strict=True):
-        home = home + shifted(block, "x", NX, NX - step).astype(jnp.float32)
-    home = lax.dot_general(
-        regroup,
-        home.astype(jnp.bfloat16).reshape(experts * 2 * GROUP, D_PART),
-        CONTRACT_ROWS,
-        preferred_element_type=jnp.float32,
-    ).astype(jnp.bfloat16)
-    home = swap(home.reshape(NY, sent, D_PART), "y").transpose(1, 0, 2).reshape(sent, D)
-    expert_out = home[:slot_count].astype(jnp.float32)
-    input_slot = home[slot_count : 2 * slot_count].astype(jnp.float32)
-    layer_out = jnp.dot(
-        picker, gate_slot[:, None] * expert_out, precision=lax.Precision.HIGHEST
-    ).astype(jnp.bfloat16)
-    gate_terms = jnp.sum(expert_out * upstream, axis=1)
-    gate_grads = jnp.dot(choose, gate_terms, precision=lax.Precision.HIGHEST).reshape(
-        tok_rows, TOPK
-    )
-    token_grads = jnp.dot(picker, input_slot, precision=lax.Precision.HIGHEST).astype(jnp.bfloat16)
+    grads, acts = lax.optimization_barrier((grads, acts))
+    grads = swap(lax.psum_scatter(grads, "z", scatter_dimension=0, tiled=True), ("x", "c"))
+    gate_weight_grads, up_weight_grads, down_weight_grads = tile_grads(grads)
+
+    layer_out, gate_grads, token_grads = 0.0, 0.0, 0.0
+    for first, count in PARTS:
+        home = send_home(outputs(slots, weights, acts, first, count), count)
+        here = slice(first * CAP, (first + count) * CAP)
+        expert_out = home[: count * CAP].astype(jnp.float32)
+        input_slot = home[count * CAP : 2 * count * CAP].astype(jnp.float32)
+        layer_out += jnp.dot(
+            picker[:, here], gate_slot[here, None] * expert_out, precision=lax.Precision.HIGHEST
+        )
+        gate_terms = jnp.sum(expert_out * upstream[here], axis=1)
+        gate_grads += jnp.dot(choose[:, here], gate_terms, precision=lax.Precision.HIGHEST)
+        token_grads += jnp.dot(picker[:, here], input_slot, precision=lax.Precision.HIGHEST)
+    layer_out = layer_out.astype(jnp.bfloat16)
+    token_grads = token_grads.astype(jnp.bfloat16)
+    gate_grads = gate_grads.reshape(tok_rows, TOPK)
     return (
         layer_out,
         token_grads,

time: 283 us -> 259 us (0.915)
  waiting for transfers between devices: 83.9 us -> 59.7 us
  Pallas kernels: 26.3 us -> 12.9 us
  starting transfers between devices: 61.8 us -> 74.2 us
    ppermute x9 -> x13, waiting for transfers between devices: 63.3 us -> 47.6 us  [shifted(): lax.ppermute(value, axis, [(i, (i + step) % size) for i in range(size)])]
    ppermute x9 -> x13, starting transfers between devices: 43.8 us -> 56.3 us  [shifted(): lax.ppermute(value, axis, [(i, (i + step) % size) for i in range(size)])]
    pallas_call x4 -> x6, Pallas kernels: 23.9 us -> 12.6 us  [the longest x2 4.32 us: outputs(): pl.pallas_call(functools.partial(output_kernel, first), grid_spec=pltpu.P...]
    all_to_all x2 -> x3, waiting for transfers between devices: 16.9 us -> 12 us  [swap(): return lax.all_to_all(value, axis, split_axis=0, concat_axis=0, tiled=True)]
    reduce_scatter x1, waiting for transfers between devices: 3.69 us -> 0.01 us  [per_device(): lax.psum_scatter(grads, 'z', scatter_dimension=0, tiled=True)]
    dot_general x4 -> x8, matrix products: 6.13 us -> 8.18 us  [the longest x2 2.95 us: per_device(): jnp.dot(picker[:, here], gate_slot[here, None] * expert_out, precision=la...]
    unnamed x54 -> x57, local copies, waits for them, and re-layouts: 14.4 us -> 14.7 us
    all_to_all x2 -> x3, starting transfers between devices: 17.9 us -> 17.8 us  [swap(): return lax.all_to_all(value, axis, split_axis=0, concat_axis=0, tiled=True)]
  transfers between devices with their start and end apart: 13 -> 18, of which waited for: 10 -> 11; matrix products, arithmetic and copies ran while one was open for 7% -> 8% of each run, Pallas kernels for 3% -> 2%
where the time goes in v3:
time: 259 us; the launch traced here: 257 us
  starting transfers between devices  74.2 us (29%)
  blocking collectives  59.8 us (23%)
  waiting for transfers between devices  59.7 us (23%)
  local copies, waits for them, and re-layouts  16.4 us (6%)
  between operations  14.7 us (6%)
  Pallas kernels  12.9 us (5%)
  matrix products  11 us (4%)
  other arithmetic  8.26 us (3%)
    all_to_all x4, blocking collectives, swap(): return lax.all_to_all(value, axis, split_axis=0, concat_axis=0, tiled=True)  59.8 us
    ppermute x13, starting transfers between devices, shifted(): lax.ppermute(value, axis, [(i, (i + step) % size) for i in range(size)])  56.3 us
    ppermute x13, waiting for transfers between devices, shifted(): lax.ppermute(value, axis, [(i, (i + step) % size) for i in range(size)])  47.6 us
    all_to_all x3, starting transfers between devices, swap(): return lax.all_to_all(value, axis, split_axis=0, concat_axis=0, tiled=True)  17.8 us
    unnamed x57, local copies, waits for them, and re-layouts  14.7 us
    all_to_all x3, waiting for transfers between devices, swap(): return lax.all_to_all(value, axis, split_axis=0, concat_axis=0, tiled=True)  12 us
  transfers between devices with their start and end apart: 18, of which 11 were waited for; matrix products, arithmetic and copies ran while one was open for 8% of the time, Pallas kernels for 2%

profile of v3, /device:TPU:1, one launch (start us, length us, event | category | flops | bytes accessed | tf_op | source)
XLA Modules:
  0.0 257.1 jit_solution(4412358694810858292)
XLA Ops:
  9.2 10.1 %all_to_all.35 = bf16[4,48,512]{2,1,0:T(8,128)(2,1)} all-to-all(bf16[4,48,512]{2,1,0:T(8,128)(2,1)} %shard_map.154), channel_id=1, replica_groups=mesh['y'=4,'c'=2,'x'=4,'z'=16] {'x'}, dimensions={0} | all-to-all | bytes 393216 | tf_op jit(solution)/shard_map/all_to_all | solution.py:44
  19.7 2.8 %reduce-window.6 = s32[10,8,128]{2,1,0:T(8,128)S(1)} reduce-window(s32[10,8,128]{2,1,0:T(8,128)S(1)} %fusion.19, s32[]{:T(128)} %constant.40.clone.1), window={size=1x1x128 pad=0_0x0_0x127_0}, to_apply=%region_0.1 | reduce-window | flops 1300480 | bytes 81924 | tf_op jit(solution)/shard_map/reduce-window
  25.7 12.8 %all_to_all.36 = bf16[4,208,512]{2,1,0:T(8,128)(2,1)S(1)} all-to-all(bf16[4,208,512]{2,1,0:T(8,128)(2,1)S(1)} %bitcast.77), channel_id=1, replica_groups=mesh['y'=4,'c'=2,'x'=4,'z'=16] {'y'}, dimensions={0} | all-to-all | bytes 1703936 | tf_op jit(solution)/shard_map/all_to_all | solution.py:44
  41.8 4.2 %collective-permute-start.1 = (bf16[10,80,512]{2,1,0:T(8,128)(2,1)S(1)}, bf16[10,80,512]{2,1,0:T(8,128)(2,1)S(1)}, u32[]{:S(2)}, u32[]{:S(2)}) collective-permute-start(bf16[10,80,512]{2,1,0:T(8,128)(2,1)S(1)} %bitcast.69), channel_id=1, source_target_pairs={{0,48},{16,0},{32,16},{48,32},{1,49},{17,1},{33,17},{49,33},{2,50}... | collective-permute-start | bytes 2457608 | tf_op jit(solution)/shard_map/ppermute | solution.py:36
  48.0 8.4 %collective-permute-done.refs_1_ = bf16[10,80,512]{2,1,0:T(8,128)(2,1)S(1)} collective-permute-done((bf16[10,80,512]{2,1,0:T(8,128)(2,1)S(1)}, bf16[10,80,512]{2,1,0:T(8,128)(2,1)S(1)}, u32[]{:S(2)}, u32[]{:S(2)}) %collective-permute-start) | collective-permute-done | bytes 819232 | tf_op jit(solution)/shard_map/ppermute | solution.py:36
  57.1 15.6 %collective-permute-done.2.refs_3_ = bf16[10,80,512]{2,1,0:T(8,128)(2,1)S(1)} collective-permute-done((bf16[10,80,512]{2,1,0:T(8,128)(2,1)S(1)}, bf16[10,80,512]{2,1,0:T(8,128)(2,1)S(1)}, u32[]{:S(2)}, u32[]{:S(2)}) %collective-permute-start.2) | collective-permute-done | bytes 819232 | tf_op jit(solution)/shard_map/ppermute | solution.py:36
  73.0 11.3 %collective-permute-start.3 = (bf16[10,160,512]{2,1,0:T(8,128)(2,1)S(1)}, bf16[10,160,512]{2,1,0:T(8,128)(2,1)S(1)}, u32[]{:S(2)}, u32[]{:S(2)}) collective-permute-start(bf16[10,160,512]{2,1,0:T(8,128)(2,1)S(1)} %get-tuple-element.23.near_inputs), channel_id=1, source_target_pairs={{0,64},{64,0},{1,65},{65,1},{2,66},{66,2},{3,67},{67,3},{4,68},{68... | collective-permute-start | bytes 4915208 | tf_op jit(solution)/shard_map/ppermute | solution.py:36
  97.3 3.0 %shard_map.156 = bf16[20,360,128]{2,1,0:T(8,128)(2,1)S(1)} custom-call(s32[60]{0:T(128)S(1)} %fusion.29.slots, bf16[64,48,512]{2,1,0:T(8,128)(2,1)S(1)} %copy-done.1, bf16[10,160,512]{2,1,0:T(8,128)(2,1)S(1)} %get-tuple-element.23.near_inputs, bf16[10,160,512]{2,1,0:T(8,128)(2,1)S(1)} %copy-done.7, bf16[10,160,512]{2,1,0:T(8,128)(2,1)S(1)} %copy-done.10, ...), custom_call_target="tpu_custom_call" | custom-call | tf_op jit(solution)/shard_map/pallas_call | solution.py:161
  100.3 17.8 %all_to_all.37 = bf16[20,360,128]{2,1,0:T(8,128)(2,1)S(1)} all-to-all(bf16[20,360,128]{2,1,0:T(8,128)(2,1)S(1)} %shard_map.156), channel_id=1, replica_groups=mesh['y'=4,'c'=2,'x'=4,'z'=16] {'y'}, dimensions={0} | all-to-all | bytes 3686400 | tf_op jit(solution)/shard_map/all_to_all | solution.py:44
  118.9 19.1 %all_to_all.38.acts.act_ref = bf16[20,360,128]{2,1,0:T(8,128)(2,1)S(1)} all-to-all(bf16[20,360,128]{2,1,0:T(8,128)(2,1)S(1)} %bitcast.73), channel_id=1, replica_groups=mesh['y'=4,'c'=2,'x'=4,'z'=16] {'y'}, dimensions={0} | all-to-all | bytes 3686400 | tf_op jit(solution)/shard_map/all_to_all | solution.py:44
  146.7 13.7 %collective-permute-start.5 = (bf16[6,320,512]{2,1,0:T(8,128)(2,1)S(1)}, bf16[6,320,512]{2,1,0:T(8,128)(2,1)S(1)}, u32[]{:S(2)}, u32[]{:S(2)}) collective-permute-start(bf16[6,320,512]{2,1,0:T(8,128)(2,1)S(1)} %get-tuple-element.27), channel_id=1, source_target_pairs={{0,64},{64,0},{1,65},{65,1},{2,66},{66,2},{3,67},{67,3},{4,68},{68... | collective-permute-start | bytes 5898248 | tf_op jit(solution)/shard_map/ppermute | solution.py:36
  164.1 3.0 %collective-permute-done.9 = bf16[4,320,512]{2,1,0:T(8,128)(2,1)S(1)} collective-permute-done((bf16[4,320,512]{2,1,0:T(8,128)(2,1)S(1)}, bf16[4,320,512]{2,1,0:T(8,128)(2,1)S(1)}, u32[]{:S(2)}, u32[]{:S(2)}) %collective-permute-start.9) | collective-permute-done | bytes 1310752 | tf_op jit(solution)/shard_map/ppermute | solution.py:36
  167.5 4.2 %collective-permute-start.10 = (bf16[4,80,512]{2,1,0:T(8,128)(2,1)S(1)}, bf16[4,80,512]{2,1,0:T(8,128)(2,1)S(1)}, u32[]{:S(2)}, u32[]{:S(2)}) collective-permute-start(bf16[4,80,512]{2,1,0:T(8,128)(2,1)S(1)} %get-tuple-element.73), channel_id=1, source_target_pairs={{0,48},{16,0},{32,16},{48,32},{1,49},{17,1},{33,17},{49,33},{2,50}... | collective-permute-start | bytes 983048 | tf_op jit(solution)/shard_map/ppermute | solution.py:36
  173.6 3.8 %collective-permute-start.12 = (bf16[4,80,512]{2,1,0:T(8,128)(2,1)S(1)}, bf16[4,80,512]{2,1,0:T(8,128)(2,1)S(1)}, u32[]{:S(2)}, u32[]{:S(2)}) collective-permute-start(bf16[4,80,512]{2,1,0:T(8,128)(2,1)S(1)} %get-tuple-element.74), channel_id=1, source_target_pairs={{0,32},{16,48},{32,0},{48,16},{1,33},{17,49},{33,1},{49,17},{2,34}... | collective-permute-start | bytes 983048 | tf_op jit(solution)/shard_map/ppermute | solution.py:36
  179.3 2.8 %collective-permute-start.6 = (bf16[6,80,512]{2,1,0:T(8,128)(2,1)}, bf16[6,80,512]{2,1,0:T(8,128)(2,1)S(1)}, u32[]{:S(2)}, u32[]{:S(2)}) collective-permute-start(bf16[6,80,512]{2,1,0:T(8,128)(2,1)} %get-tuple-element.70), channel_id=1, source_target_pairs={{0,48},{16,0},{32,16},{48,32},{1,49},{17,1},{33,17},{49,33},{2,50}... | collective-permute-start | bytes 1474568 | tf_op jit(solution)/shard_map/ppermute | solution.py:36
  182.1 2.6 %collective-permute-start.7 = (bf16[6,80,512]{2,1,0:T(8,128)(2,1)}, bf16[6,80,512]{2,1,0:T(8,128)(2,1)}, u32[]{:S(2)}, u32[]{:S(2)}) collective-permute-start(bf16[6,80,512]{2,1,0:T(8,128)(2,1)} %get-tuple-element.72), channel_id=1, source_target_pairs={{0,16},{16,32},{32,48},{48,0},{1,17},{17,33},{33,49},{49,1},{2,18}... | collective-permute-start | bytes 1474568 | tf_op jit(solution)/shard_map/ppermute | solution.py:36
  184.8 3.7 %collective-permute-start.8 = (bf16[6,80,512]{2,1,0:T(8,128)(2,1)S(1)}, bf16[6,80,512]{2,1,0:T(8,128)(2,1)}, u32[]{:S(2)}, u32[]{:S(2)}) collective-permute-start(bf16[6,80,512]{2,1,0:T(8,128)(2,1)S(1)} %get-tuple-element.71), channel_id=1, source_target_pairs={{0,32},{16,48},{32,0},{48,16},{1,33},{17,49},{33,1},{49,17},{2,34}... | collective-permute-start | bytes 1474568 | tf_op jit(solution)/shard_map/ppermute | solution.py:36
  191.3 3.6 %all-to-all-start.5 = ((bf16[4,80,512]{2,1,0:T(8,128)(2,1)}), bf16[4,80,512]{2,1,0:T(8,128)(2,1)S(1)}, u32[]{:S(2)}, u32[]{:S(2)}) async-start(bf16[4,80,512]{2,1,0:T(8,128)(2,1)} %bitcast.16), calls=%async_computation.5 | async-start | bytes 655360 | tf_op jit(solution)/shard_map/all_to_all | solution.py:44
  194.9 2.6 %collective-permute-done.6 = bf16[6,80,512]{2,1,0:T(8,128)(2,1)S(1)} collective-permute-done((bf16[6,80,512]{2,1,0:T(8,128)(2,1)}, bf16[6,80,512]{2,1,0:T(8,128)(2,1)S(1)}, u32[]{:S(2)}, u32[]{:S(2)}) %collective-permute-start.6) | collective-permute-done | bytes 491552 | tf_op jit(solution)/shard_map/ppermute | solution.py:36
  197.6 14.6 %collective-permute-done.7 = bf16[6,80,512]{2,1,0:T(8,128)(2,1)} collective-permute-done((bf16[6,80,512]{2,1,0:T(8,128)(2,1)}, bf16[6,80,512]{2,1,0:T(8,128)(2,1)}, u32[]{:S(2)}, u32[]{:S(2)}) %collective-permute-start.7) | collective-permute-done | bytes 491552 | tf_op jit(solution)/shard_map/ppermute | solution.py:36
  215.2 3.6 %all-to-all-start.4 = ((bf16[4,128,512]{2,1,0:T(8,128)(2,1)}), bf16[4,128,512]{2,1,0:T(8,128)(2,1)S(1)}, u32[]{:S(2)}, u32[]{:S(2)}) async-start(bf16[4,128,512]{2,1,0:T(8,128)(2,1)} %bitcast.12), calls=%async_computation.4 | async-start | bytes 1048576 | tf_op jit(solution)/shard_map/all_to_all | solution.py:44
  219.5 7.5 %all-to-all-done.4 = bf16[4,128,512]{2,1,0:T(8,128)(2,1)S(1)} async-done(((bf16[4,128,512]{2,1,0:T(8,128)(2,1)}), bf16[4,128,512]{2,1,0:T(8,128)(2,1)S(1)}, u32[]{:S(2)}, u32[]{:S(2)}) %all-to-all-start.4) | async-done | bytes 524320 | tf_op jit(solution)/shard_map/all_to_all | solution.py:44
  233.0 10.7 %all-to-all-start.6 = ((bf16[8,48,256]{2,1,0:T(8,128)(2,1)}), bf16[8,48,256]{2,1,0:T(8,128)(2,1)S(1)}, u32[]{:S(2)}, u32[]{:S(2)}) async-start(bf16[8,48,256]{2,1,0:T(8,128)(2,1)} %reduce-scatter.2.cloned.1.call-done), calls=%async_computation.7 | async-start | bytes 393216 | tf_op jit(solution)/shard_map/all_to_all | solution.py:44
  245.1 4.4 %all-to-all-done.6.parts = bf16[8,48,256]{2,1,0:T(8,128)(2,1)S(1)} async-done(((bf16[8,48,256]{2,1,0:T(8,128)(2,1)}), bf16[8,48,256]{2,1,0:T(8,128)(2,1)S(1)}, u32[]{:S(2)}, u32[]{:S(2)}) %all-to-all-start.6) | async-done | bytes 196640 | tf_op jit(solution)/shard_map/all_to_all | solution.py:44
  (134 shorter events, 56.4 us)
Async XLA Ops:
  7.2 83.9 %all-gather.2.cloned.1.call-start = ((), (), s32[]{:S(2)}) async-start(), calls=%async_computation.8 | async-start | bytes 3342336 | tf_op jit(solution)/shard_map/all_gather | solution.py:317
  19.4 213.6 %reduce-scatter.2.cloned.1.call-start = ((), (), s32[]{:S(2)}) async-start(), calls=%async_computation.9 | async-start | bytes 3342336 | tf_op jit(solution)/shard_map/reduce_scatter | solution.py:374
  39.5 47.9 %copy-start.22 = (s32[60]{0:T(128)S(1)}, s32[60]{0:T(128)}, u32[]{:S(2)}) copy-start(s32[60]{0:T(128)} %param.14) | copy-start | bytes 724
  39.5 16.9 %collective-permute-start = (bf16[10,80,512]{2,1,0:T(8,128)(2,1)S(1)}, bf16[10,80,512]{2,1,0:T(8,128)(2,1)S(1)}, u32[]{:S(2)}, u32[]{:S(2)}) collective-permute-start(bf16[10,80,512]{2,1,0:T(8,128)(2,1)S(1)} %bitcast.68), channel_id=1, source_target_pairs={{0,16},{16,32},{32,48},{48,0},{1,17},{17,33},{33,49},{49,1},{2,18}... | collective-permute-start | bytes 2457608 | tf_op jit(solution)/shard_map/ppermute | solution.py:36
  41.8 15.3 %collective-permute-start.1 = (bf16[10,80,512]{2,1,0:T(8,128)(2,1)S(1)}, bf16[10,80,512]{2,1,0:T(8,128)(2,1)S(1)}, u32[]{:S(2)}, u32[]{:S(2)}) collective-permute-start(bf16[10,80,512]{2,1,0:T(8,128)(2,1)S(1)} %bitcast.69), channel_id=1, source_target_pairs={{0,48},{16,0},{32,16},{48,32},{1,49},{17,1},{33,17},{49,33},{2,50}... | collective-permute-start | bytes 2457608 | tf_op jit(solution)/shard_map/ppermute | solution.py:36
  46.0 26.7 %collective-permute-start.2 = (bf16[10,80,512]{2,1,0:T(8,128)(2,1)S(1)}, bf16[10,80,512]{2,1,0:T(8,128)(2,1)S(1)}, u32[]{:S(2)}, u32[]{:S(2)}) collective-permute-start(bf16[10,80,512]{2,1,0:T(8,128)(2,1)S(1)} %bitcast.70), channel_id=1, source_target_pairs={{0,32},{16,48},{32,0},{48,16},{1,33},{17,49},{33,1},{49,17},{2,34}... | collective-permute-start | bytes 2457608 | tf_op jit(solution)/shard_map/ppermute | solution.py:36
  73.0 27.3 %copy-start.4 = (bf16[10,160,512]{2,1,0:T(8,128)(2,1)}, bf16[10,160,512]{2,1,0:T(8,128)(2,1)S(1)}, u32[]{:S(2)}) copy-start(bf16[10,160,512]{2,1,0:T(8,128)(2,1)S(1)} %get-tuple-element.23.near_inputs) | copy-start | bytes 4915204
  73.0 14.4 %collective-permute-start.3 = (bf16[10,160,512]{2,1,0:T(8,128)(2,1)S(1)}, bf16[10,160,512]{2,1,0:T(8,128)(2,1)S(1)}, u32[]{:S(2)}, u32[]{:S(2)}) collective-permute-start(bf16[10,160,512]{2,1,0:T(8,128)(2,1)S(1)} %get-tuple-element.23.near_inputs), channel_id=1, source_target_pairs={{0,64},{64,0},{1,65},{65,1},{2,66},{66,2},{3,67},{67,3},{4,68},{68... | collective-permute-start | bytes 4915208 | tf_op jit(solution)/shard_map/ppermute | solution.py:36
  84.3 5.5 %collective-permute-start.4 = (bf16[10,160,512]{2,1,0:T(8,128)(2,1)S(1)}, bf16[10,160,512]{2,1,0:T(8,128)(2,1)S(1)}, u32[]{:S(2)}, u32[]{:S(2)}) collective-permute-start(bf16[10,160,512]{2,1,0:T(8,128)(2,1)S(1)} %get-tuple-element.24.near_scaled), channel_id=1, source_target_pairs={{0,64},{64,0},{1,65},{65,1},{2,66},{66,2},{3,67},{67,3},{4,68},{68... | collective-permute-start | bytes 4915208 | tf_op jit(solution)/shard_map/ppermute | solution.py:36
  118.6 19.4 %copy-start.14 = (bf16[10,160,512]{2,1,0:T(8,128)(2,1)S(1)}, bf16[10,160,512]{2,1,0:T(8,128)(2,1)}, u32[]{:S(2)}) copy-start(bf16[10,160,512]{2,1,0:T(8,128)(2,1)} %copy-done.12) | copy-start | bytes 4915204
  118.6 19.4 %copy-start.11 = (bf16[10,160,512]{2,1,0:T(8,128)(2,1)S(1)}, bf16[10,160,512]{2,1,0:T(8,128)(2,1)}, u32[]{:S(2)}) copy-start(bf16[10,160,512]{2,1,0:T(8,128)(2,1)} %copy-done.9) | copy-start | bytes 4915204
  118.9 19.1 %copy-start.5 = (bf16[10,160,512]{2,1,0:T(8,128)(2,1)S(1)}, bf16[10,160,512]{2,1,0:T(8,128)(2,1)}, u32[]{:S(2)}) copy-start(bf16[10,160,512]{2,1,0:T(8,128)(2,1)} %copy-done.4) | copy-start | bytes 4915204
  146.7 31.1 %collective-permute-start.5 = (bf16[6,320,512]{2,1,0:T(8,128)(2,1)S(1)}, bf16[6,320,512]{2,1,0:T(8,128)(2,1)S(1)}, u32[]{:S(2)}, u32[]{:S(2)}) collective-permute-start(bf16[6,320,512]{2,1,0:T(8,128)(2,1)S(1)} %get-tuple-element.27), channel_id=1, source_target_pairs={{0,64},{64,0},{1,65},{65,1},{2,66},{66,2},{3,67},{67,3},{4,68},{68... | collective-permute-start | bytes 5898248 | tf_op jit(solution)/shard_map/ppermute | solution.py:36
  162.2 4.9 %collective-permute-start.9 = (bf16[4,320,512]{2,1,0:T(8,128)(2,1)S(1)}, bf16[4,320,512]{2,1,0:T(8,128)(2,1)S(1)}, u32[]{:S(2)}, u32[]{:S(2)}) collective-permute-start(bf16[4,320,512]{2,1,0:T(8,128)(2,1)S(1)} %get-tuple-element.32), channel_id=1, source_target_pairs={{0,64},{64,0},{1,65},{65,1},{2,66},{66,2},{3,67},{67,3},{4,68},{68... | collective-permute-start | bytes 3932168 | tf_op jit(solution)/shard_map/ppermute | solution.py:36
  167.5 17.3 %collective-permute-start.10 = (bf16[4,80,512]{2,1,0:T(8,128)(2,1)S(1)}, bf16[4,80,512]{2,1,0:T(8,128)(2,1)S(1)}, u32[]{:S(2)}, u32[]{:S(2)}) collective-permute-start(bf16[4,80,512]{2,1,0:T(8,128)(2,1)S(1)} %get-tuple-element.73), channel_id=1, source_target_pairs={{0,48},{16,0},{32,16},{48,32},{1,49},{17,1},{33,17},{49,33},{2,50}... | collective-permute-start | bytes 983048 | tf_op jit(solution)/shard_map/ppermute | solution.py:36
  171.7 16.8 %collective-permute-start.11 = (bf16[4,80,512]{2,1,0:T(8,128)(2,1)S(1)}, bf16[4,80,512]{2,1,0:T(8,128)(2,1)S(1)}, u32[]{:S(2)}, u32[]{:S(2)}) collective-permute-start(bf16[4,80,512]{2,1,0:T(8,128)(2,1)S(1)} %get-tuple-element.75), channel_id=1, source_target_pairs={{0,16},{16,32},{32,48},{48,0},{1,17},{17,33},{33,49},{49,1},{2,18}... | collective-permute-start | bytes 983048 | tf_op jit(solution)/shard_map/ppermute | solution.py:36
  173.6 16.4 %collective-permute-start.12 = (bf16[4,80,512]{2,1,0:T(8,128)(2,1)S(1)}, bf16[4,80,512]{2,1,0:T(8,128)(2,1)S(1)}, u32[]{:S(2)}, u32[]{:S(2)}) collective-permute-start(bf16[4,80,512]{2,1,0:T(8,128)(2,1)S(1)} %get-tuple-element.74), channel_id=1, source_target_pairs={{0,32},{16,48},{32,0},{48,16},{1,33},{17,49},{33,1},{49,17},{2,34}... | collective-permute-start | bytes 983048 | tf_op jit(solution)/shard_map/ppermute | solution.py:36
  179.3 18.2 %collective-permute-start.6 = (bf16[6,80,512]{2,1,0:T(8,128)(2,1)}, bf16[6,80,512]{2,1,0:T(8,128)(2,1)S(1)}, u32[]{:S(2)}, u32[]{:S(2)}) collective-permute-start(bf16[6,80,512]{2,1,0:T(8,128)(2,1)} %get-tuple-element.70), channel_id=1, source_target_pairs={{0,48},{16,0},{32,16},{48,32},{1,49},{17,1},{33,17},{49,33},{2,50}... | collective-permute-start | bytes 1474568 | tf_op jit(solution)/shard_map/ppermute | solution.py:36
  182.1 30.0 %collective-permute-start.7 = (bf16[6,80,512]{2,1,0:T(8,128)(2,1)}, bf16[6,80,512]{2,1,0:T(8,128)(2,1)}, u32[]{:S(2)}, u32[]{:S(2)}) collective-permute-start(bf16[6,80,512]{2,1,0:T(8,128)(2,1)} %get-tuple-element.72), channel_id=1, source_target_pairs={{0,16},{16,32},{32,48},{48,0},{1,17},{17,33},{33,49},{49,1},{2,18}... | collective-permute-start | bytes 1474568 | tf_op jit(solution)/shard_map/ppermute | solution.py:36
  184.8 27.4 %collective-permute-start.8 = (bf16[6,80,512]{2,1,0:T(8,128)(2,1)S(1)}, bf16[6,80,512]{2,1,0:T(8,128)(2,1)}, u32[]{:S(2)}, u32[]{:S(2)}) collective-permute-start(bf16[6,80,512]{2,1,0:T(8,128)(2,1)S(1)} %get-tuple-element.71), channel_id=1, source_target_pairs={{0,32},{16,48},{32,0},{48,16},{1,33},{17,49},{33,1},{49,17},{2,34}... | collective-permute-start | bytes 1474568 | tf_op jit(solution)/shard_map/ppermute | solution.py:36
  191.3 22.6 %copy-start.18 = (bf16[480,512]{1,0:T(8,128)(2,1)S(1)}, bf16[480,512]{1,0:T(8,128)(2,1)}, u32[]{:S(2)}) copy-start(bf16[480,512]{1,0:T(8,128)(2,1)} %constant.51.clone) | copy-start | bytes 1474564
  191.3 23.9 %all-to-all-start.5 = ((bf16[4,80,512]{2,1,0:T(8,128)(2,1)}), bf16[4,80,512]{2,1,0:T(8,128)(2,1)S(1)}, u32[]{:S(2)}, u32[]{:S(2)}) async-start(bf16[4,80,512]{2,1,0:T(8,128)(2,1)} %bitcast.16), calls=%async_computation.5 | async-start | bytes 655360 | tf_op jit(solution)/shard_map/all_to_all | solution.py:44
  215.2 11.9 %all-to-all-start.4 = ((bf16[4,128,512]{2,1,0:T(8,128)(2,1)}), bf16[4,128,512]{2,1,0:T(8,128)(2,1)S(1)}, u32[]{:S(2)}, u32[]{:S(2)}) async-start(bf16[4,128,512]{2,1,0:T(8,128)(2,1)} %bitcast.12), calls=%async_computation.4 | async-start | bytes 1048576 | tf_op jit(solution)/shard_map/all_to_all | solution.py:44
  233.0 16.5 %all-to-all-start.6 = ((bf16[8,48,256]{2,1,0:T(8,128)(2,1)}), bf16[8,48,256]{2,1,0:T(8,128)(2,1)S(1)}, u32[]{:S(2)}, u32[]{:S(2)}) async-start(bf16[8,48,256]{2,1,0:T(8,128)(2,1)} %reduce-scatter.2.cloned.1.call-done), calls=%async_computation.7 | async-start | bytes 393216 | tf_op jit(solution)/shard_map/all_to_all | solution.py:44
  (18 other events, 123.6 us)
Sparse Core Ops, SparseCore 0:
  19.5 71.5 all-gather.1
  142.4 87.2 reduce-scatter.1

commit v4 on v3

--- a/solution.py
+++ b/solution.py
@@ -372,23 +372,27 @@
     grads = weight_grads(slots, acts, rows, experts, z_count * NX)
     grads, acts = lax.optimization_barrier((grads, acts))
     grads = swap(lax.psum_scatter(grads, "z", scatter_dimension=0, tiled=True), ("x", "c"))
-    gate_weight_grads, up_weight_grads, down_weight_grads = tile_grads(grads)
-
     layer_out, gate_grads, token_grads = 0.0, 0.0, 0.0
     for first, count in PARTS:
         home = send_home(outputs(slots, weights, acts, first, count), count)
         here = slice(first * CAP, (first + count) * CAP)
         expert_out = home[: count * CAP].astype(jnp.float32)
-        input_slot = home[count * CAP : 2 * count * CAP].astype(jnp.float32)
-        layer_out += jnp.dot(
-            picker[:, here], gate_slot[here, None] * expert_out, precision=lax.Precision.HIGHEST
+        gated = (gate_slot[here, None] * expert_out).astype(jnp.bfloat16)
+        layer_out += jnp.dot(picker_half[:, here], gated, preferred_element_type=jnp.float32)
+        token_grads += jnp.dot(
+            picker_half[:, here],
+            home[count * CAP : 2 * count * CAP],
+            preferred_element_type=jnp.float32,
         )
         gate_terms = jnp.sum(expert_out * upstream[here], axis=1)
-        gate_grads += jnp.dot(choose[:, here], gate_terms, precision=lax.Precision.HIGHEST)
-        token_grads += jnp.dot(picker[:, here], input_slot, precision=lax.Precision.HIGHEST)
+        gate_grads += jnp.sum(choose[:, here] * gate_terms[None, :], axis=1)
     layer_out = layer_out.astype(jnp.bfloat16)
     token_grads = token_grads.astype(jnp.bfloat16)
     gate_grads = gate_grads.reshape(tok_rows, TOPK)
+    grads, layer_out, token_grads, gate_grads = lax.optimization_barrier(
+        (grads, layer_out, token_grads, gate_grads)
+    )
+    gate_weight_grads, up_weight_grads, down_weight_grads = tile_grads(grads)
     return (
         layer_out,
         token_grads,

time: 259 us -> 258 us (level)
  matrix products: 11 us -> 8.06 us
    dot_general x6 -> x4, matrix products: 5.81 us -> 2.94 us  [the longest x2 1.5 us: per_device(): jnp.dot(picker_half[:, here], gated, preferred_element_type=jnp.float32)]
  transfers between devices with their start and end apart: 18 -> 18, of which waited for: 11 -> 11; matrix products, arithmetic and copies ran while one was open for 8% -> 7% of each run, Pallas kernels for 2% -> 2%
where the time goes in v4:
time: 258 us; the launch traced here: 257 us
  starting transfers between devices  76 us (29%)
  waiting for transfers between devices  61 us (24%)
  blocking collectives  59.9 us (23%)
  local copies, waits for them, and re-layouts  16.4 us (6%)
  between operations  14.7 us (6%)
  Pallas kernels  12.9 us (5%)
  other arithmetic  8.38 us (3%)
  matrix products  8.06 us (3%)
    all_to_all x4, blocking collectives, swap(): return lax.all_to_all(value, axis, split_axis=0, concat_axis=0, tiled=True)  59.9 us
    ppermute x13, starting transfers between devices, shifted(): lax.ppermute(value, axis, [(i, (i + step) % size) for i in range(size)])  56.1 us
    ppermute x13, waiting for transfers between devices, shifted(): lax.ppermute(value, axis, [(i, (i + step) % size) for i in range(size)])  47.5 us
    all_to_all x3, starting transfers between devices, swap(): return lax.all_to_all(value, axis, split_axis=0, concat_axis=0, tiled=True)  19.8 us
    unnamed x57, local copies, waits for them, and re-layouts  14.7 us
    all_to_all x3, waiting for transfers between devices, swap(): return lax.all_to_all(value, axis, split_axis=0, concat_axis=0, tiled=True)  13.1 us
  transfers between devices with their start and end apart: 18, of which 11 were waited for; matrix products, arithmetic and copies ran while one was open for 7% of the time, Pallas kernels for 2%

profile of v4, /device:TPU:1, one launch (start us, length us, event | category | flops | bytes accessed | tf_op | source)
XLA Modules:
  0.0 257.3 jit_solution(18129288838051577111)
XLA Ops:
  9.2 10.1 %all_to_all.35 = bf16[4,48,512]{2,1,0:T(8,128)(2,1)} all-to-all(bf16[4,48,512]{2,1,0:T(8,128)(2,1)} %shard_map.154), channel_id=1, replica_groups=mesh['y'=4,'c'=2,'x'=4,'z'=16] {'x'}, dimensions={0} | all-to-all | bytes 393216 | tf_op jit(solution)/shard_map/all_to_all | solution.py:44
  19.7 2.8 %reduce-window.6 = s32[10,8,128]{2,1,0:T(8,128)S(1)} reduce-window(s32[10,8,128]{2,1,0:T(8,128)S(1)} %fusion.17, s32[]{:T(128)} %constant.39.clone.1), window={size=1x1x128 pad=0_0x0_0x127_0}, to_apply=%region_0.1 | reduce-window | flops 1300480 | bytes 81924 | tf_op jit(solution)/shard_map/reduce-window
  25.6 12.8 %all_to_all.36 = bf16[4,208,512]{2,1,0:T(8,128)(2,1)S(1)} all-to-all(bf16[4,208,512]{2,1,0:T(8,128)(2,1)S(1)} %bitcast.71), channel_id=1, replica_groups=mesh['y'=4,'c'=2,'x'=4,'z'=16] {'y'}, dimensions={0} | all-to-all | bytes 1703936 | tf_op jit(solution)/shard_map/all_to_all | solution.py:44
  41.7 4.2 %collective-permute-start.1 = (bf16[10,80,512]{2,1,0:T(8,128)(2,1)S(1)}, bf16[10,80,512]{2,1,0:T(8,128)(2,1)S(1)}, u32[]{:S(2)}, u32[]{:S(2)}) collective-permute-start(bf16[10,80,512]{2,1,0:T(8,128)(2,1)S(1)} %bitcast.63), channel_id=1, source_target_pairs={{0,48},{16,0},{32,16},{48,32},{1,49},{17,1},{33,17},{49,33},{2,50}... | collective-permute-start | bytes 2457608 | tf_op jit(solution)/shard_map/ppermute | solution.py:36
  47.9 8.4 %collective-permute-done.refs_1_ = bf16[10,80,512]{2,1,0:T(8,128)(2,1)S(1)} collective-permute-done((bf16[10,80,512]{2,1,0:T(8,128)(2,1)S(1)}, bf16[10,80,512]{2,1,0:T(8,128)(2,1)S(1)}, u32[]{:S(2)}, u32[]{:S(2)}) %collective-permute-start) | collective-permute-done | bytes 819232 | tf_op jit(solution)/shard_map/ppermute | solution.py:36
  57.0 15.6 %collective-permute-done.2.refs_3_ = bf16[10,80,512]{2,1,0:T(8,128)(2,1)S(1)} collective-permute-done((bf16[10,80,512]{2,1,0:T(8,128)(2,1)S(1)}, bf16[10,80,512]{2,1,0:T(8,128)(2,1)S(1)}, u32[]{:S(2)}, u32[]{:S(2)}) %collective-permute-start.2) | collective-permute-done | bytes 819232 | tf_op jit(solution)/shard_map/ppermute | solution.py:36
  72.9 11.3 %collective-permute-start.3 = (bf16[10,160,512]{2,1,0:T(8,128)(2,1)S(1)}, bf16[10,160,512]{2,1,0:T(8,128)(2,1)S(1)}, u32[]{:S(2)}, u32[]{:S(2)}) collective-permute-start(bf16[10,160,512]{2,1,0:T(8,128)(2,1)S(1)} %get-tuple-element.27.near_inputs), channel_id=1, source_target_pairs={{0,64},{64,0},{1,65},{65,1},{2,66},{66,2},{3,67},{67,3},{4,68},{68... | collective-permute-start | bytes 4915208 | tf_op jit(solution)/shard_map/ppermute | solution.py:36
  97.3 3.0 %shard_map.156 = bf16[20,360,128]{2,1,0:T(8,128)(2,1)S(1)} custom-call(s32[60]{0:T(128)S(1)} %fusion.24.slots, bf16[64,48,512]{2,1,0:T(8,128)(2,1)S(1)} %copy-done.1, bf16[10,160,512]{2,1,0:T(8,128)(2,1)S(1)} %get-tuple-element.27.near_inputs, bf16[10,160,512]{2,1,0:T(8,128)(2,1)S(1)} %copy-done.7, bf16[10,160,512]{2,1,0:T(8,128)(2,1)S(1)} %copy-done.10, ...), custom_call_target="tpu_custom_call" | custom-call | tf_op jit(solution)/shard_map/pallas_call | solution.py:161
  100.3 17.8 %all_to_all.37 = bf16[20,360,128]{2,1,0:T(8,128)(2,1)S(1)} all-to-all(bf16[20,360,128]{2,1,0:T(8,128)(2,1)S(1)} %shard_map.156), channel_id=1, replica_groups=mesh['y'=4,'c'=2,'x'=4,'z'=16] {'y'}, dimensions={0} | all-to-all | bytes 3686400 | tf_op jit(solution)/shard_map/all_to_all | solution.py:44
  118.9 19.2 %all_to_all.38.acts.act_ref = bf16[20,360,128]{2,1,0:T(8,128)(2,1)S(1)} all-to-all(bf16[20,360,128]{2,1,0:T(8,128)(2,1)S(1)} %bitcast.67), channel_id=1, replica_groups=mesh['y'=4,'c'=2,'x'=4,'z'=16] {'y'}, dimensions={0} | all-to-all | bytes 3686400 | tf_op jit(solution)/shard_map/all_to_all | solution.py:44
  138.1 2.6 %shard_map.157 = bf16[128,48,256]{2,1,0:T(8,128)(2,1)S(1)} custom-call(s32[60]{0:T(128)S(1)} %fusion.24.slots, bf16[20,360,128]{2,1,0:T(8,128)(2,1)S(1)} %all_to_all.38.acts.act_ref, bf16[10,160,512]{2,1,0:T(8,128)(2,1)S(1)} %copy-done.5, bf16[10,160,512]{2,1,0:T(8,128)(2,1)S(1)} %copy-done.8, bf16[10,160,512]{2,1,0:T(8,128)(2,1)S(1)} %copy-done.11, ...), custom_call_target="tpu_custom_call" | custom-call | tf_op jit(solution)/shard_map/pallas_call | solution.py:207
  146.8 13.9 %collective-permute-start.5 = (bf16[6,320,512]{2,1,0:T(8,128)(2,1)S(1)}, bf16[6,320,512]{2,1,0:T(8,128)(2,1)S(1)}, u32[]{:S(2)}, u32[]{:S(2)}) collective-permute-start(bf16[6,320,512]{2,1,0:T(8,128)(2,1)S(1)} %get-tuple-element.32), channel_id=1, source_target_pairs={{0,64},{64,0},{1,65},{65,1},{2,66},{66,2},{3,67},{67,3},{4,68},{68... | collective-permute-start | bytes 5898248 | tf_op jit(solution)/shard_map/ppermute | solution.py:36
  164.4 3.0 %collective-permute-done.9 = bf16[4,320,512]{2,1,0:T(8,128)(2,1)S(1)} collective-permute-done((bf16[4,320,512]{2,1,0:T(8,128)(2,1)S(1)}, bf16[4,320,512]{2,1,0:T(8,128)(2,1)S(1)}, u32[]{:S(2)}, u32[]{:S(2)}) %collective-permute-start.9) | collective-permute-done | bytes 1310752 | tf_op jit(solution)/shard_map/ppermute | solution.py:36
  167.7 3.8 %collective-permute-start.10 = (bf16[4,80,512]{2,1,0:T(8,128)(2,1)S(1)}, bf16[4,80,512]{2,1,0:T(8,128)(2,1)S(1)}, u32[]{:S(2)}, u32[]{:S(2)}) collective-permute-start(bf16[4,80,512]{2,1,0:T(8,128)(2,1)S(1)} %get-tuple-element.81), channel_id=1, source_target_pairs={{0,48},{16,0},{32,16},{48,32},{1,49},{17,1},{33,17},{49,33},{2,50}... | collective-permute-start | bytes 983048 | tf_op jit(solution)/shard_map/ppermute | solution.py:36
  173.5 3.9 %collective-permute-start.12 = (bf16[4,80,512]{2,1,0:T(8,128)(2,1)S(1)}, bf16[4,80,512]{2,1,0:T(8,128)(2,1)S(1)}, u32[]{:S(2)}, u32[]{:S(2)}) collective-permute-start(bf16[4,80,512]{2,1,0:T(8,128)(2,1)S(1)} %get-tuple-element.82), channel_id=1, source_target_pairs={{0,32},{16,48},{32,0},{48,16},{1,33},{17,49},{33,1},{49,17},{2,34}... | collective-permute-start | bytes 983048 | tf_op jit(solution)/shard_map/ppermute | solution.py:36
  179.4 2.7 %collective-permute-start.6 = (bf16[6,80,512]{2,1,0:T(8,128)(2,1)}, bf16[6,80,512]{2,1,0:T(8,128)(2,1)S(1)}, u32[]{:S(2)}, u32[]{:S(2)}) collective-permute-start(bf16[6,80,512]{2,1,0:T(8,128)(2,1)} %get-tuple-element.78), channel_id=1, source_target_pairs={{0,48},{16,0},{32,16},{48,32},{1,49},{17,1},{33,17},{49,33},{2,50}... | collective-permute-start | bytes 1474568 | tf_op jit(solution)/shard_map/ppermute | solution.py:36
  182.1 2.7 %collective-permute-start.7 = (bf16[6,80,512]{2,1,0:T(8,128)(2,1)}, bf16[6,80,512]{2,1,0:T(8,128)(2,1)}, u32[]{:S(2)}, u32[]{:S(2)}) collective-permute-start(bf16[6,80,512]{2,1,0:T(8,128)(2,1)} %get-tuple-element.80), channel_id=1, source_target_pairs={{0,16},{16,32},{32,48},{48,0},{1,17},{17,33},{33,49},{49,1},{2,18}... | collective-permute-start | bytes 1474568 | tf_op jit(solution)/shard_map/ppermute | solution.py:36
  184.9 3.6 %collective-permute-start.8 = (bf16[6,80,512]{2,1,0:T(8,128)(2,1)}, bf16[6,80,512]{2,1,0:T(8,128)(2,1)}, u32[]{:S(2)}, u32[]{:S(2)}) collective-permute-start(bf16[6,80,512]{2,1,0:T(8,128)(2,1)} %get-tuple-element.79), channel_id=1, source_target_pairs={{0,32},{16,48},{32,0},{48,16},{1,33},{17,49},{33,1},{49,17},{2,34}... | collective-permute-start | bytes 1474568 | tf_op jit(solution)/shard_map/ppermute | solution.py:36
  191.3 3.6 %all-to-all-start.6 = ((bf16[4,80,512]{2,1,0:T(8,128)(2,1)}), bf16[4,80,512]{2,1,0:T(8,128)(2,1)S(1)}, u32[]{:S(2)}, u32[]{:S(2)}) async-start(bf16[4,80,512]{2,1,0:T(8,128)(2,1)} %bitcast.16), calls=%async_computation.7 | async-start | bytes 655360 | tf_op jit(solution)/shard_map/all_to_all | solution.py:44
  197.5 14.7 %collective-permute-done.7 = bf16[6,80,512]{2,1,0:T(8,128)(2,1)} collective-permute-done((bf16[6,80,512]{2,1,0:T(8,128)(2,1)}, bf16[6,80,512]{2,1,0:T(8,128)(2,1)}, u32[]{:S(2)}, u32[]{:S(2)}) %collective-permute-start.7) | collective-permute-done | bytes 491552 | tf_op jit(solution)/shard_map/ppermute | solution.py:36
  215.1 3.6 %all-to-all-start.5 = ((bf16[4,128,512]{2,1,0:T(8,128)(2,1)}), bf16[4,128,512]{2,1,0:T(8,128)(2,1)S(1)}, u32[]{:S(2)}, u32[]{:S(2)}) async-start(bf16[4,128,512]{2,1,0:T(8,128)(2,1)} %bitcast.12), calls=%async_computation.6 | async-start | bytes 1048576 | tf_op jit(solution)/shard_map/all_to_all | solution.py:44
  219.1 8.3 %all-to-all-done.5 = bf16[4,128,512]{2,1,0:T(8,128)(2,1)S(1)} async-done(((bf16[4,128,512]{2,1,0:T(8,128)(2,1)}), bf16[4,128,512]{2,1,0:T(8,128)(2,1)S(1)}, u32[]{:S(2)}, u32[]{:S(2)}) %all-to-all-start.5) | async-done | bytes 524320 | tf_op jit(solution)/shard_map/all_to_all | solution.py:44
  230.6 12.6 %all-to-all-start.4 = ((bf16[8,48,256]{2,1,0:T(8,128)(2,1)}), bf16[8,48,256]{2,1,0:T(8,128)(2,1)S(1)}, u32[]{:S(2)}, u32[]{:S(2)}) async-start(bf16[8,48,256]{2,1,0:T(8,128)(2,1)} %reduce-scatter.2.cloned.1.call-done), calls=%async_computation.5 | async-start | bytes 393216 | tf_op jit(solution)/shard_map/all_to_all | solution.py:44
  244.3 4.8 %all-to-all-done.4.parts = bf16[8,48,256]{2,1,0:T(8,128)(2,1)S(1)} async-done(((bf16[8,48,256]{2,1,0:T(8,128)(2,1)}), bf16[8,48,256]{2,1,0:T(8,128)(2,1)S(1)}, u32[]{:S(2)}, u32[]{:S(2)}) %all-to-all-start.4) | async-done | bytes 196640 | tf_op jit(solution)/shard_map/all_to_all | solution.py:44
  (134 shorter events, 53.6 us)
Async XLA Ops:
  7.2 83.9 %all-gather.2.cloned.1.call-start = ((), (), s32[]{:S(2)}) async-start(), calls=%async_computation.8 | async-start | bytes 3342336 | tf_op jit(solution)/shard_map/all_gather | solution.py:317
  19.4 211.2 %reduce-scatter.2.cloned.1.call-start = ((), (), s32[]{:S(2)}) async-start(), calls=%async_computation.9 | async-start | bytes 3342336 | tf_op jit(solution)/shard_map/reduce_scatter | solution.py:374
  39.4 47.9 %copy-start.22 = (s32[60]{0:T(128)S(1)}, s32[60]{0:T(128)}, u32[]{:S(2)}) copy-start(s32[60]{0:T(128)} %param.14) | copy-start | bytes 724
  39.4 16.9 %collective-permute-start = (bf16[10,80,512]{2,1,0:T(8,128)(2,1)S(1)}, bf16[10,80,512]{2,1,0:T(8,128)(2,1)S(1)}, u32[]{:S(2)}, u32[]{:S(2)}) collective-permute-start(bf16[10,80,512]{2,1,0:T(8,128)(2,1)S(1)} %bitcast.62), channel_id=1, source_target_pairs={{0,16},{16,32},{32,48},{48,0},{1,17},{17,33},{33,49},{49,1},{2,18}... | collective-permute-start | bytes 2457608 | tf_op jit(solution)/shard_map/ppermute | solution.py:36
  41.7 15.3 %collective-permute-start.1 = (bf16[10,80,512]{2,1,0:T(8,128)(2,1)S(1)}, bf16[10,80,512]{2,1,0:T(8,128)(2,1)S(1)}, u32[]{:S(2)}, u32[]{:S(2)}) collective-permute-start(bf16[10,80,512]{2,1,0:T(8,128)(2,1)S(1)} %bitcast.63), channel_id=1, source_target_pairs={{0,48},{16,0},{32,16},{48,32},{1,49},{17,1},{33,17},{49,33},{2,50}... | collective-permute-start | bytes 2457608 | tf_op jit(solution)/shard_map/ppermute | solution.py:36
  45.9 26.7 %collective-permute-start.2 = (bf16[10,80,512]{2,1,0:T(8,128)(2,1)S(1)}, bf16[10,80,512]{2,1,0:T(8,128)(2,1)S(1)}, u32[]{:S(2)}, u32[]{:S(2)}) collective-permute-start(bf16[10,80,512]{2,1,0:T(8,128)(2,1)S(1)} %bitcast.64), channel_id=1, source_target_pairs={{0,32},{16,48},{32,0},{48,16},{1,33},{17,49},{33,1},{49,17},{2,34}... | collective-permute-start | bytes 2457608 | tf_op jit(solution)/shard_map/ppermute | solution.py:36
  72.9 27.4 %copy-start.4 = (bf16[10,160,512]{2,1,0:T(8,128)(2,1)}, bf16[10,160,512]{2,1,0:T(8,128)(2,1)S(1)}, u32[]{:S(2)}) copy-start(bf16[10,160,512]{2,1,0:T(8,128)(2,1)S(1)} %get-tuple-element.27.near_inputs) | copy-start | bytes 4915204
  72.9 14.4 %collective-permute-start.3 = (bf16[10,160,512]{2,1,0:T(8,128)(2,1)S(1)}, bf16[10,160,512]{2,1,0:T(8,128)(2,1)S(1)}, u32[]{:S(2)}, u32[]{:S(2)}) collective-permute-start(bf16[10,160,512]{2,1,0:T(8,128)(2,1)S(1)} %get-tuple-element.27.near_inputs), channel_id=1, source_target_pairs={{0,64},{64,0},{1,65},{65,1},{2,66},{66,2},{3,67},{67,3},{4,68},{68... | collective-permute-start | bytes 4915208 | tf_op jit(solution)/shard_map/ppermute | solution.py:36
  84.2 5.5 %collective-permute-start.4 = (bf16[10,160,512]{2,1,0:T(8,128)(2,1)S(1)}, bf16[10,160,512]{2,1,0:T(8,128)(2,1)S(1)}, u32[]{:S(2)}, u32[]{:S(2)}) collective-permute-start(bf16[10,160,512]{2,1,0:T(8,128)(2,1)S(1)} %get-tuple-element.28.near_scaled), channel_id=1, source_target_pairs={{0,64},{64,0},{1,65},{65,1},{2,66},{66,2},{3,67},{67,3},{4,68},{68... | collective-permute-start | bytes 4915208 | tf_op jit(solution)/shard_map/ppermute | solution.py:36
  118.6 19.6 %copy-start.14 = (bf16[10,160,512]{2,1,0:T(8,128)(2,1)S(1)}, bf16[10,160,512]{2,1,0:T(8,128)(2,1)}, u32[]{:S(2)}) copy-start(bf16[10,160,512]{2,1,0:T(8,128)(2,1)} %copy-done.12) | copy-start | bytes 4915204
  118.6 19.5 %copy-start.11 = (bf16[10,160,512]{2,1,0:T(8,128)(2,1)S(1)}, bf16[10,160,512]{2,1,0:T(8,128)(2,1)}, u32[]{:S(2)}) copy-start(bf16[10,160,512]{2,1,0:T(8,128)(2,1)} %copy-done.9) | copy-start | bytes 4915204
  118.9 19.3 %copy-start.5 = (bf16[10,160,512]{2,1,0:T(8,128)(2,1)S(1)}, bf16[10,160,512]{2,1,0:T(8,128)(2,1)}, u32[]{:S(2)}) copy-start(bf16[10,160,512]{2,1,0:T(8,128)(2,1)} %copy-done.4) | copy-start | bytes 4915204
  146.8 30.8 %collective-permute-start.5 = (bf16[6,320,512]{2,1,0:T(8,128)(2,1)S(1)}, bf16[6,320,512]{2,1,0:T(8,128)(2,1)S(1)}, u32[]{:S(2)}, u32[]{:S(2)}) collective-permute-start(bf16[6,320,512]{2,1,0:T(8,128)(2,1)S(1)} %get-tuple-element.32), channel_id=1, source_target_pairs={{0,64},{64,0},{1,65},{65,1},{2,66},{66,2},{3,67},{67,3},{4,68},{68... | collective-permute-start | bytes 5898248 | tf_op jit(solution)/shard_map/ppermute | solution.py:36
  162.5 4.9 %collective-permute-start.9 = (bf16[4,320,512]{2,1,0:T(8,128)(2,1)S(1)}, bf16[4,320,512]{2,1,0:T(8,128)(2,1)S(1)}, u32[]{:S(2)}, u32[]{:S(2)}) collective-permute-start(bf16[4,320,512]{2,1,0:T(8,128)(2,1)S(1)} %get-tuple-element.37), channel_id=1, source_target_pairs={{0,64},{64,0},{1,65},{65,1},{2,66},{66,2},{3,67},{67,3},{4,68},{68... | collective-permute-start | bytes 3932168 | tf_op jit(solution)/shard_map/ppermute | solution.py:36
  167.7 17.1 %collective-permute-start.10 = (bf16[4,80,512]{2,1,0:T(8,128)(2,1)S(1)}, bf16[4,80,512]{2,1,0:T(8,128)(2,1)S(1)}, u32[]{:S(2)}, u32[]{:S(2)}) collective-permute-start(bf16[4,80,512]{2,1,0:T(8,128)(2,1)S(1)} %get-tuple-element.81), channel_id=1, source_target_pairs={{0,48},{16,0},{32,16},{48,32},{1,49},{17,1},{33,17},{49,33},{2,50}... | collective-permute-start | bytes 983048 | tf_op jit(solution)/shard_map/ppermute | solution.py:36
  171.6 16.9 %collective-permute-start.11 = (bf16[4,80,512]{2,1,0:T(8,128)(2,1)S(1)}, bf16[4,80,512]{2,1,0:T(8,128)(2,1)S(1)}, u32[]{:S(2)}, u32[]{:S(2)}) collective-permute-start(bf16[4,80,512]{2,1,0:T(8,128)(2,1)S(1)} %get-tuple-element.83), channel_id=1, source_target_pairs={{0,16},{16,32},{32,48},{48,0},{1,17},{17,33},{33,49},{49,1},{2,18}... | collective-permute-start | bytes 983048 | tf_op jit(solution)/shard_map/ppermute | solution.py:36
  173.5 16.5 %collective-permute-start.12 = (bf16[4,80,512]{2,1,0:T(8,128)(2,1)S(1)}, bf16[4,80,512]{2,1,0:T(8,128)(2,1)S(1)}, u32[]{:S(2)}, u32[]{:S(2)}) collective-permute-start(bf16[4,80,512]{2,1,0:T(8,128)(2,1)S(1)} %get-tuple-element.82), channel_id=1, source_target_pairs={{0,32},{16,48},{32,0},{48,16},{1,33},{17,49},{33,1},{49,17},{2,34}... | collective-permute-start | bytes 983048 | tf_op jit(solution)/shard_map/ppermute | solution.py:36
  179.4 18.0 %collective-permute-start.6 = (bf16[6,80,512]{2,1,0:T(8,128)(2,1)}, bf16[6,80,512]{2,1,0:T(8,128)(2,1)S(1)}, u32[]{:S(2)}, u32[]{:S(2)}) collective-permute-start(bf16[6,80,512]{2,1,0:T(8,128)(2,1)} %get-tuple-element.78), channel_id=1, source_target_pairs={{0,48},{16,0},{32,16},{48,32},{1,49},{17,1},{33,17},{49,33},{2,50}... | collective-permute-start | bytes 1474568 | tf_op jit(solution)/shard_map/ppermute | solution.py:36
  182.1 30.0 %collective-permute-start.7 = (bf16[6,80,512]{2,1,0:T(8,128)(2,1)}, bf16[6,80,512]{2,1,0:T(8,128)(2,1)}, u32[]{:S(2)}, u32[]{:S(2)}) collective-permute-start(bf16[6,80,512]{2,1,0:T(8,128)(2,1)} %get-tuple-element.80), channel_id=1, source_target_pairs={{0,16},{16,32},{32,48},{48,0},{1,17},{17,33},{33,49},{49,1},{2,18}... | collective-permute-start | bytes 1474568 | tf_op jit(solution)/shard_map/ppermute | solution.py:36
  184.9 27.3 %collective-permute-start.8 = (bf16[6,80,512]{2,1,0:T(8,128)(2,1)}, bf16[6,80,512]{2,1,0:T(8,128)(2,1)}, u32[]{:S(2)}, u32[]{:S(2)}) collective-permute-start(bf16[6,80,512]{2,1,0:T(8,128)(2,1)} %get-tuple-element.79), channel_id=1, source_target_pairs={{0,32},{16,48},{32,0},{48,16},{1,33},{17,49},{33,1},{49,17},{2,34}... | collective-permute-start | bytes 1474568 | tf_op jit(solution)/shard_map/ppermute | solution.py:36
  191.3 22.5 %copy-start.18 = (bf16[480,512]{1,0:T(8,128)(2,1)S(1)}, bf16[480,512]{1,0:T(8,128)(2,1)}, u32[]{:S(2)}) copy-start(bf16[480,512]{1,0:T(8,128)(2,1)} %constant.51.clone) | copy-start | bytes 1474564
  191.3 23.8 %all-to-all-start.6 = ((bf16[4,80,512]{2,1,0:T(8,128)(2,1)}), bf16[4,80,512]{2,1,0:T(8,128)(2,1)S(1)}, u32[]{:S(2)}, u32[]{:S(2)}) async-start(bf16[4,80,512]{2,1,0:T(8,128)(2,1)} %bitcast.16), calls=%async_computation.7 | async-start | bytes 655360 | tf_op jit(solution)/shard_map/all_to_all | solution.py:44
  215.1 12.3 %all-to-all-start.5 = ((bf16[4,128,512]{2,1,0:T(8,128)(2,1)}), bf16[4,128,512]{2,1,0:T(8,128)(2,1)S(1)}, u32[]{:S(2)}, u32[]{:S(2)}) async-start(bf16[4,128,512]{2,1,0:T(8,128)(2,1)} %bitcast.12), calls=%async_computation.6 | async-start | bytes 1048576 | tf_op jit(solution)/shard_map/all_to_all | solution.py:44
  230.6 18.5 %all-to-all-start.4 = ((bf16[8,48,256]{2,1,0:T(8,128)(2,1)}), bf16[8,48,256]{2,1,0:T(8,128)(2,1)S(1)}, u32[]{:S(2)}, u32[]{:S(2)}) async-start(bf16[8,48,256]{2,1,0:T(8,128)(2,1)} %reduce-scatter.2.cloned.1.call-done), calls=%async_computation.5 | async-start | bytes 393216 | tf_op jit(solution)/shard_map/all_to_all | solution.py:44
  (18 other events, 123.7 us)
Sparse Core Ops, SparseCore 0:
  19.5 71.6 all-gather.1
  142.6 86.7 reduce-scatter.1
